TPU v7x, 512 devices: a whole 4x4x16 slice. The times are simulated.
512 devices in a mesh: dp: 8 (over y, core), vocab: 64 (over z, x).
Axes of the slice: x: 4, y: 4, z: 16, core: 2. Of those that a mesh axis runs over, the one named last changes fastest.
Arguments:
- hidden: bfloat16 [384, 4096], P('dp'), may hold values from -30 to 30
- head_weight: bfloat16 [131072, 4096], P('vocab', 'dp'), may hold values from -0.375 to 0.375
- teacher_ids: int32 [384, 256], P('dp'), may hold values from 0 to 131071
- teacher_logits: float32 [384, 256], P('dp'), may hold values from -16 to 16
Outputs:
- hidden_grad: bfloat16 [384, 4096], P('dp', 'vocab')
- head_grad: bfloat16 [131072, 4096], P('vocab', 'dp')
- loss: float32 [], replicated
All inputs are finite; a program needn't handle non-finite values.
Results may differ from a plain program's by a relative error of at most 0.0049.
Values may be sent and summed in bfloat16 or wider, within the bound.
A program may use at most 64 MiB of HBM per device.

v0:
```python
import jax
import jax.numpy as jnp
from jax import lax
from jax.sharding import PartitionSpec as P

soft_cap = 30.0


def build_target(ids, prob, first_entry, vocab_span):
    row_count = ids.shape[0]
    local_ids = ids - first_entry
    inside = (local_ids >= 0) & (local_ids < vocab_span)
    row_index = lax.broadcasted_iota(jnp.int32, ids.shape, 0)
    flat_place = jnp.where(inside, row_index * vocab_span + local_ids, row_count * vocab_span)
    return (
        jnp.zeros((row_count * vocab_span,), jnp.float32)
        .at[flat_place.reshape(-1)]
        .add(prob.reshape(-1), mode="drop")
        .reshape(row_count, vocab_span)
    )


def teacher_terms(logits):
    logp = logits - jnp.log(jnp.sum(jnp.exp(logits), axis=1, keepdims=True))
    return (logp, jnp.exp(logp))


def per_device(hidden, head_weight, teacher_ids, teacher_logits):
    tok_dp = hidden.shape[0]
    vocab_span = head_weight.shape[0]
    first_entry = lax.axis_index("vocab") * vocab_span
    columns = lax.all_to_all(hidden, "dp", split_axis=1, concat_axis=0, tiled=True)
    partial_value = lax.dot_general(
        columns, head_weight, (((1,), (1,)), ((), ())), preferred_element_type=jnp.float32
    )
    raw = lax.psum_scatter(partial_value, "dp", scatter_dimension=0, tiled=True)
    row_logp, row_prob = teacher_terms(teacher_logits)
    target = build_target(teacher_ids, row_prob, first_entry, vocab_span)
    squash = jnp.tanh(raw / soft_cap)
    student = soft_cap * squash
    expo = jnp.exp(student)
    total, cross = lax.psum((jnp.sum(expo, axis=1), jnp.sum(target * student, axis=1)), "vocab")
    token_loss = jnp.sum(row_prob * row_logp, axis=1) - cross + jnp.log(total)
    grad_raw = ((expo / total[:, None] - target) * (1.0 - squash * squash)).astype(jnp.bfloat16)
    loss = lax.psum(jnp.sum(token_loss), "dp") / (tok_dp * lax.axis_size("dp"))
    every_grad = lax.all_gather(grad_raw, "dp", axis=0, tiled=True)
    head_grad = lax.dot_general(
        every_grad, columns, (((0,), (0,)), ((), ())), preferred_element_type=jnp.float32
    )
    grad_terms = jnp.dot(every_grad, head_weight, preferred_element_type=jnp.float32)
    token_terms = lax.all_to_all(grad_terms, "dp", split_axis=0, concat_axis=1, tiled=True)
    hidden_grad = lax.psum_scatter(token_terms, "vocab", scatter_dimension=1, tiled=True)
    return (hidden_grad.astype(jnp.bfloat16), head_grad.astype(jnp.bfloat16), loss)


def solution(mesh):
    in_specs = (P("dp", None), P("vocab", "dp"), P("dp", None), P("dp", None))
    out_specs = (P("dp", "vocab"), P("vocab", "dp"), P())
    return jax.shard_map(
        per_device, mesh=mesh, in_specs=in_specs, out_specs=out_specs, check_vma=False
    )
```

profile of v0, /device:TPU:16, one launch (start us, length us, event | category | flops | bytes accessed | tf_op | source)
XLA Modules:
  0.0 988.8 jit_solution(5568715171707308050)
XLA Ops:
  7.2 0.0 copy-start
  7.2 0.0 reduce-scatter.5.cloned.1.call-start
  7.2 1.2 copy.21
  8.4 14.3 %all_to_all.38 = bf16[48,8,512]{2,0,1:T(8,128)(2,1)S(1)} all-to-all(bf16[48,8,512]{2,0,1:T(8,128)(2,1)S(1)} %bitcast.30), channel_id=1, replica_groups=mesh['dp'=8,'vocab'=64] {'dp'}, dimensions={1} | all-to-all | bytes 786432 | tf_op jit(solution)/shard_map/all_to_all | solution.py:32
  22.7 0.0 copy-done
  22.7 2.7 fusion.3
  25.4 0.0 reduce-scatter.5.cloned.1.call-update
  25.4 0.0 all-gather.2.cloned.1.call-start
  25.5 0.7 copy-done.2
  26.2 0.1 select_bitcast_fusion
  26.3 0.1 copy.18
  26.3 0.1 exponential_reduce_fusion.1
  26.5 0.2 fusion.2
  26.7 0.1 compare_select_fusion
  26.8 64.6 %scatter_custom_fusion = f32[98304]{0:T(1024)S(1)} fusion(s32[12288]{0:T(1024)S(1)} %bitcast.37, f32[12288]{0:T(1024)S(1)} %bitcast.36, f32[]{:T(128)} %constant.11.clone.1), kind=kCustom, calls=%fused_computation.8 | custom fusion | flops 12288 | bytes 393220 | tf_op jit(solution)/shard_map/scatter-add | solution.py:18
  91.4 0.1 reshape.56
  91.4 0.0 reduce-scatter.5.cloned.1.call-done
  91.5 1.2 multiply_reduce_fusion
  92.7 146.1 %all-reduce = (f32[48]{0:T(128)S(1)}, f32[48]{0:T(128)S(1)}) all-reduce(f32[48]{0:T(128)S(1)} %get-tuple-element.4, f32[48]{0:T(128)S(1)} %get-tuple-element.3), channel_id=1, replica_groups=mesh['dp'=8,'vocab'=64] {'vocab'}, use_global_device_ids=true, to_apply=%region_2.3 | all-reduce | flops 96 | bytes 768 | tf_op jit(solution)/shard_map/psum | solution.py:42
  238.8 1.8 multiply_convert_fusion
  240.7 0.0 all-gather.2.cloned.1.call-update
  240.7 0.0 reduce-scatter.7.cloned.1.call-start
  240.8 23.8 %all-gather.2.cloned.1.call-done = bf16[384,2048]{1,0:T(8,128)(2,1)} async-done(((bf16[48,2048]{1,0:T(8,128)(2,1)}), bf16[384,2048]{1,0:T(8,128)(2,1)}) %all-gather.2.cloned.1.call-update) | async-done | bytes 1572880 | tf_op jit(solution)/shard_map/all_gather | solution.py:46
  264.6 2.4 fusion.4
  267.0 14.7 %all_to_all.39 = f32[8,48,512]{2,1,0:T(8,128)S(1)} all-to-all(f32[8,48,512]{2,1,0:T(8,128)S(1)} %bitcast.33), channel_id=1, replica_groups=mesh['dp'=8,'vocab'=64] {'dp'}, dimensions={0} | all-to-all | bytes 1572864 | tf_op jit(solution)/shard_map/all_to_all | solution.py:51
  281.7 2.0 copy.15
  283.6 0.0 reduce-scatter.7.cloned.1.call-update
  283.6 0.6 add_reduce_fusion
  284.3 12.0 %psum.23 = f32[]{:T(128)} all-reduce(f32[]{:T(128)} %add_reduce_fusion), channel_id=1, replica_groups=mesh['dp'=8,'vocab'=64] {'dp'}, use_global_device_ids=true, to_apply=%region_10.11 | all-reduce | flops 1 | bytes 8 | tf_op jit(solution)/shard_map/psum | solution.py:45
  296.9 4.0 convolution_convert_fusion
  300.9 678.8 %reduce-scatter.7.cloned.1.call-done = f32[64,48]{1,0:T(8,128)} async-done(((f32[4096,48]{1,0:T(8,128)}), f32[64,48]{1,0:T(8,128)}) %reduce-scatter.7.cloned.1.call-update) | async-done | bytes 12304
  979.7 1.4 copy.14
  (6 shorter events, 0.0 us)
Async XLA Ops:
  7.2 15.6 %copy-start = (bf16[2048,512]{1,0:T(8,128)(2,1)S(1)}, bf16[2048,512]{1,0:T(8,128)(2,1)}, u32[]{:S(2)}) copy-start(bf16[2048,512]{1,0:T(8,128)(2,1)} %param.5) | copy-start | bytes 6291460
  7.2 84.3 %reduce-scatter.5.cloned.1.call-start = ((), (), s32[]{:S(2)}) async-start(), calls=%async_computation.4 | async-start | bytes 3538944 | tf_op jit(solution)/shard_map/reduce_scatter | solution.py:36
  25.4 0.8 copy-start.2
  25.4 0.9 copy-start.1
  25.4 239.2 %all-gather.2.cloned.1.call-start = ((), (), s32[]{:S(2)}) async-start(), calls=%async_computation.5 | async-start | bytes 1769472 | tf_op jit(solution)/shard_map/all_gather | solution.py:46
  240.7 739.0 %reduce-scatter.7.cloned.1.call-start = ((), (), s32[]{:S(2)}) async-start(), calls=%async_computation.6 | async-start | bytes 2129920
Sparse Core Ops, SparseCore 0:
  25.6 39.6 reduce-scatter.4
  240.8 23.7 all-gather.1
  283.8 695.8 reduce-scatter.6
where the time goes:
time: 989 us
  waiting for transfers between devices  703 us (71%)
  blocking collectives  187 us (19%)
  other arithmetic  68.7 us (7%)
  between operations  15.6 us (2%)
    unnamed x4, waiting for transfers between devices  679 us
    psum x1, blocking collectives, per_device(): lax.psum((jnp.sum(expo, axis=1), jnp.sum(target * student, axis=1)), 'voc...  146 us
    scatter-add x1, other arithmetic, build_target(): return jnp.zeros((row_count * vocab_span,), jnp.float32).at[flat_place.re...  64.6 us
    all_gather x1, waiting for transfers between devices, per_device(): every_grad = lax.all_gather(grad_raw, 'dp', axis=0, tiled=True)  23.8 us
  transfers between devices with their start and end apart: 3, of which 2 were waited for; matrix products, arithmetic and copies ran while one was open for 7% of the time, Pallas kernels for 0%

commit v1 on v0

v1 whole, which is shorter than its diff:
```python
import jax
import jax.numpy as jnp
from jax import lax
from jax.experimental import pallas as pl
from jax.experimental.pallas import tpu as pltpu
from jax.sharding import PartitionSpec as P

MESH = pl.DeviceIdType.MESH
F32 = jnp.float32
BF16 = jnp.bfloat16
soft_cap = 30.0

NY, NC, NX, NZ = 4, 2, 4, 16
TOK, D, K = 48, 4096, 256
FEAT = D // 8
VOCAB = 131072 // 64
NQ = 4
QC = VOCAB // NQ
NHI = VOCAB // 128
BEND = 48.0
LEVELS = 32767.0


def encode(x):
    return jnp.round(x * (LEVELS / (jnp.abs(x) + BEND))).astype(jnp.int32).astype(jnp.int16)


def decode(q):
    u = q.astype(jnp.int32).astype(F32)
    return u * (BEND / (LEVELS - jnp.abs(u)))


def mm(a, b, ca, cb):
    return lax.dot_general(a, b, (((ca,), (cb,)), ((), ())), preferred_element_type=F32)


def kernel(
    hidden, weight, ids, logits, out_hidden, out_head, out_loss,
    wv, hv, psib, pown, srecv, enc_opp, enc_nb, in_opp, in_nb,
    prob, tgt, es, om, psx, psz, lossb, gv, gt, xs, xr, zs, zr, fin, fin_in, head,
    w_sem, own_sem, hs_sem, hr_sem, ss_sem, sr_sem, rs_s, rs_r,
    px_s, px_r, pz_s, pz_r, ls_s, ls_r, ag_s, ag_r, x_s, x_r, z_s, z_r, f_s, f_r, head_sem,
):
    me = lax.axis_index("dp")
    vo = lax.axis_index("vocab")
    y, c = me // 2, me % 2
    z, x = vo // NX, vo % NX

    def dp_dev(o, cx):
        return {"dp": ((y + o) % NY) * 2 + (c + cx) % 2, "vocab": vo}

    def x_dev(r):
        return {"dp": me, "vocab": z * NX + (x + r) % NX}

    def z_dev(zz):
        return {"dp": me, "vocab": zz * NX + x}

    def rc(src, dst, ssem, rsem, dev):
        return pltpu.make_async_remote_copy(
            src_ref=src, dst_ref=dst, send_sem=ssem, recv_sem=rsem, device_id=dev, device_id_type=MESH
        )

    waits = []

    def send(src, dst, ssem, rsem, dev):
        copy = rc(src, dst, ssem, rsem, dev)
        copy.start()
        waits.append(copy)

    def wait_recv(dst, ssem, rsem):
        rc(dst, dst, ssem, rsem, dp_dev(0, 1)).wait_recv()

    sends_final = z % 2 == c
    fin_block = z // 2
    dest_v = [8 * me + 2 * x + h for h in range(2)]
    dest_self = [jnp.logical_and(fin_block == me, v == vo) for v in dest_v]
    src_dp = vo // 8
    src_v = (2 * me + src_dp % 2) * NX + (vo % 8) // 2
    src_self = jnp.logical_and(src_dp == me, src_v == vo)

    wcopies = []
    for q in range(NQ):
        rows = pl.ds(q * QC, QC)
        wcopies.append(pltpu.make_async_copy(weight.at[rows], wv.at[rows], w_sem.at[q]))
    own_h = pltpu.make_async_copy(hidden.at[:, pl.ds(pl.multiple_of(me * FEAT, FEAT), FEAT)], hv.at[0, 0], own_sem)
    own_h.start()
    for w in wcopies:
        w.start()

    barrier = pltpu.get_barrier_semaphore()

    def greet(dev):
        pl.semaphore_signal(barrier, inc=1, device_id=dev, device_id_type=MESH)

    for o in range(NY):
        for cx in range(NC):
            if o or cx:
                greet(dp_dev(o, cx))
    for r in range(1, NX):
        greet(x_dev(r))
    for r in range(1, NZ):
        greet(z_dev((z + r) % NZ))

    @pl.when(jnp.logical_not(src_self))
    def _():
        greet({"dp": src_dp, "vocab": src_v})

    extra = jnp.where(
        sends_final, 2 - dest_self[0].astype(jnp.int32) - dest_self[1].astype(jnp.int32), 0
    )
    pl.semaphore_wait(barrier, 7 + (NX - 1) + (NZ - 1) + extra)

    for o, cx in ((2, 0), (2, 1), (1, 0), (3, 0), (1, 1), (3, 1), (0, 1)):
        dev = dp_dev(o, cx)
        back = (-o) % NY
        cols = pl.ds(pl.multiple_of(dev["dp"] * FEAT, FEAT), FEAT)
        send(hidden.at[:, cols], hv.at[back, cx], hs_sem.at[o, cx], hr_sem.at[back, cx], dev)

    lg = logits[...]
    logp = lg - jnp.log(jnp.sum(jnp.exp(lg), axis=1, keepdims=True))
    pr = jnp.exp(logp)
    prob[...] = pr
    entropy = jnp.sum(pr * logp, axis=1, keepdims=True)

    for q in range(NQ):
        wcopies[q].wait()
    for o in range(NY):
        wait_recv(hv.at[o, 1], hs_sem.at[o, 1], hr_sem.at[o, 1])

    def q_of(s):
        return (s % 2) * 2 + s // 2

    def sib_copy(q):
        return rc(psib.at[q], srecv.at[q], ss_sem.at[q], sr_sem.at[q], dp_dev(0, 1))

    @pl.loop(0, NQ)
    def _(s):
        q = q_of(s)
        hb = hv[:, 1].reshape(NY * TOK, FEAT)
        part = mm(hb, wv[pl.ds(pl.multiple_of(q * QC, QC), QC), :], 1, 1)
        psib[q] = part.reshape(NY, TOK, QC)
        sib_copy(q).start()

    own_h.wait()
    for o in range(1, NY):
        wait_recv(hv.at[o, 0], hs_sem.at[o, 0], hr_sem.at[o, 0])

    def way(q):
        return 1 + 2 * (q // 2)

    def opp_copy(q):
        return rc(enc_opp.at[q], in_opp.at[q], rs_s.at[0, q], rs_r.at[0, q], dp_dev(way(q), 0))

    def nb_copy(q, o):
        slot, back = o // 2, 1 - o // 2
        return rc(enc_nb.at[q, slot], in_nb.at[q, back], rs_s.at[1 + slot, q], rs_r.at[1 + back, q], dp_dev(o, 0))

    @pl.loop(0, NQ)
    def _(s):
        q = q_of(s)
        hb = hv[:, 0].reshape(NY * TOK, FEAT)
        part = mm(hb, wv[pl.ds(pl.multiple_of(q * QC, QC), QC), :], 1, 1)
        pown[q] = part.reshape(NY, TOK, QC)
        wait_recv(srecv.at[q], ss_sem.at[q], sr_sem.at[q])
        enc_opp[q] = encode(pown[q, 2] + srecv[q, 2])
        opp_copy(q).start()
        other = 4 - way(q)
        enc_nb[q, other // 2] = encode(pown[q, other] + srecv[q, other])
        nb_copy(q, other).start()

    @pl.loop(0, NQ)
    def _(s):
        q = q_of(s)
        wait_recv(in_opp.at[q], rs_s.at[0, q], rs_r.at[0, q])
        o = way(q)
        enc_nb[q, o // 2] = encode(pown[q, o] + srecv[q, o] + decode(in_opp[q]))
        nb_copy(q, o).start()

    first = vo * VOCAB
    rows16 = lax.broadcasted_iota(jnp.int32, (NHI, K), 0)
    rows128 = lax.broadcasted_iota(jnp.int32, (128, K), 0)

    @pl.loop(0, TOK)
    def _(t):
        place = ids[pl.ds(t, 1), :] - first
        p = prob[pl.ds(t, 1), :]
        a = jnp.where((place >> 7) == rows16, p, 0.0)
        a1 = a.astype(BF16)
        rest = a - a1.astype(F32)
        a2 = rest.astype(BF16)
        a3 = (rest - a2.astype(F32)).astype(BF16)
        b = jnp.where((place & 127) == rows128, 1.0, 0.0).astype(BF16)
        both = mm(jnp.concatenate([a1, a2, a3], axis=0), b, 1, 1)
        tgt[t] = both[0:NHI] + both[NHI:2 * NHI] + both[2 * NHI:3 * NHI]

    tot = jnp.zeros((TOK, 128), F32)
    crs = jnp.zeros((TOK, 128), F32)
    for s in range(NQ):
        q = q_of(s)
        for slot in range(2):
            wait_recv(in_nb.at[q, slot], rs_s.at[1 + slot, q], rs_r.at[1 + slot, q])
        for k in range(QC // 128):
            cols = slice(k * 128, (k + 1) * 128)
            hi = q * (QC // 128) + k
            raw = (
                pown[q, 0, :, cols] + srecv[q, 0, :, cols]
                + decode(in_nb[q, 0, :, cols]) + decode(in_nb[q, 1, :, cols])
            )
            squash = jnp.tanh(raw * (1.0 / soft_cap))
            student = soft_cap * squash
            expo = jnp.exp(student)
            es[hi] = expo
            om[hi] = 1.0 - squash * squash
            tot = tot + expo
            crs = crs + tgt[:, hi, :] * student

    lane = lax.broadcasted_iota(jnp.int32, (TOK, 128), 1)
    row = lax.broadcasted_iota(jnp.int32, (TOK, 128), 0)
    mine = jnp.where(lane == row, jnp.sum(tot, axis=1, keepdims=True), 0.0) + jnp.where(
        lane == row + 64, jnp.sum(crs, axis=1, keepdims=True), 0.0
    )
    psx[x] = jnp.sum(mine, axis=0, keepdims=True)
    for r in range(1, NX):
        send(psx.at[x], psx.at[x], px_s.at[r], px_r.at[x], x_dev(r))
    for r in range(1, NX):
        src = (x + r) % NX
        wait_recv(psx.at[src], px_s.at[r], px_r.at[src])
    psz[z] = psx[0] + psx[1] + psx[2] + psx[3]
    for r in range(1, NZ):
        send(psz.at[z], psz.at[z], pz_s.at[r], pz_r.at[z], z_dev((z + r) % NZ))
    for r in range(1, NZ):
        src = (z + r) % NZ
        wait_recv(psz.at[src], pz_s.at[r], pz_r.at[src])
    sums = psz[0]
    for k in range(1, NZ):
        sums = sums + psz[k]
    sums = jnp.broadcast_to(sums, (TOK, 128))
    total = jnp.sum(jnp.where(lane == row, sums, 0.0), axis=1, keepdims=True)
    cross = jnp.sum(jnp.where(lane == row + 64, sums, 0.0), axis=1, keepdims=True)
    inv = 1.0 / total
    for hi in range(NHI):
        g = (es[hi] * inv - tgt[:, hi, :]) * om[hi]
        gv[0, 0, :, hi * 128:(hi + 1) * 128] = g.astype(BF16)

    half = [pl.ds(0, VOCAB // 2), pl.ds(VOCAB // 2, VOCAB // 2)]

    def pass_on(n, o, h, do, dcx):
        back = (o - do) % NY
        src = gv.at[o, 0] if h is None else gv.at[o, 0, :, half[h]]
        dst = gv.at[back, dcx] if h is None else gv.at[back, dcx, :, half[h]]
        send(src, dst, ag_s.at[n], ag_r.at[n], dp_dev(do, dcx))

    def arrived(n, o, cx, h):
        dst = gv.at[o, cx] if h is None else gv.at[o, cx, :, half[h]]
        wait_recv(dst, ag_s.at[n], ag_r.at[n])

    pass_on(0, 0, 0, 1, 0)
    pass_on(1, 0, 1, 3, 0)
    pass_on(2, 0, None, 0, 1)
    pass_on(3, 0, 1, 1, 0)
    pass_on(4, 0, 0, 3, 0)

    token_loss = entropy - cross + jnp.log(total)
    lossb[me] = jnp.broadcast_to(jnp.sum(token_loss, axis=0, keepdims=True), (1, 128))
    for o in range(NY):
        for cx in range(NC):
            if o or cx:
                dev = dp_dev(o, cx)
                send(lossb.at[me], lossb.at[me], ls_s.at[o * 2 + cx], ls_r.at[me], dev)

    def terms(o):
        ga = gv[o].reshape(2 * TOK, VOCAB)
        for n in range(2):
            part = mm(ga, wv[:, n * 256:(n + 1) * 256], 1, 0)
            for m in range(2):
                piece = part[:, m * 128:(m + 1) * 128]
                gt[o, 2 * n + m] = piece
                xs[o, 2 * n + m] = piece.astype(BF16)
        for r in range(1, NX):
            there = (x + r) % NX
            send(xs.at[o, there], xr.at[o, (-r) % NX - 1], x_s.at[o, r - 1], x_r.at[o, (-r) % NX - 1], x_dev(r))

    zsends = []

    def to_z(o):
        for r in range(NX - 1):
            wait_recv(xr.at[o, r], x_s.at[o, r], x_r.at[o, r])
        val = gt[o, x]
        for r in range(NX - 1):
            val = val + xr[o, r].astype(F32)
        for cx in range(NC):
            i = ((y + o) % NY) * 2 + (c + cx) % 2
            zd = 2 * i + c
            r = (z - zd + NZ) % NZ
            zs[o, cx] = val[cx * TOK:(cx + 1) * TOK].astype(BF16)
            copy = rc(zs.at[o, cx], zr.at[r], z_s.at[o, cx], z_r.at[r], z_dev(zd))

            @pl.when(r != 0)
            def _():
                copy.start()

            zsends.append((r, copy))

            @pl.when(r == 0)
            def _():
                zr[0] = zs[o, cx]

    arrived(2, 0, 1, None)
    terms(0)
    arrived(0, 3, 0, 0)
    pass_on(5, 3, 0, 1, 0)
    pass_on(7, 3, 0, 0, 1)
    arrived(1, 1, 0, 1)
    pass_on(6, 1, 1, 3, 0)
    pass_on(8, 1, 1, 0, 1)
    arrived(3, 3, 0, 1)
    pass_on(9, 3, 1, 0, 1)
    arrived(4, 1, 0, 0)
    pass_on(10, 1, 0, 0, 1)
    arrived(8, 1, 1, 1)
    arrived(10, 1, 1, 0)
    terms(1)
    to_z(0)
    arrived(7, 3, 1, 0)
    arrived(9, 3, 1, 1)
    terms(3)
    to_z(1)
    arrived(5, 2, 0, 0)
    pass_on(11, 2, 0, 0, 1)
    arrived(6, 2, 0, 1)
    pass_on(12, 2, 1, 0, 1)
    arrived(11, 2, 1, 0)
    arrived(12, 2, 1, 1)
    terms(2)
    to_z(3)

    HB = 256

    def head_copy(n):
        rows = pl.ds(pl.multiple_of(n * HB, HB), HB)
        return pltpu.make_async_copy(head.at[rows], out_head.at[rows], head_sem.at[n])

    def head_part(low, high):
        @pl.loop(low, high)
        def _(n):
            rows = pl.ds(pl.multiple_of(n * HB, HB), HB)
            ga = gv[:, :, :, rows].reshape(8 * TOK, HB)
            hb = hv[...].reshape(8 * TOK, FEAT)
            head[rows, :] = mm(ga, hb, 0, 0).astype(BF16)
            head_copy(n).start()

    nh = VOCAB // HB
    head_part(0, nh // 2)
    to_z(2)
    head_part(nh // 2, nh)

    @pl.when(sends_final)
    def _():
        acc = zr[0].astype(F32)
        for r in range(1, NZ):
            wait_recv(zr.at[r], f_s.at[0], z_r.at[r])
            acc = acc + zr[r].astype(F32)
        fin[...] = acc.astype(BF16)
        for h in range(2):
            copy = rc(fin, fin_in, f_s.at[h], f_r, {"dp": fin_block, "vocab": dest_v[h]})

            @pl.when(jnp.logical_not(dest_self[h]))
            def _():
                copy.start()

            @pl.when(dest_self[h])
            def _():
                fin_in[...] = fin[...]

    for o in range(NY):
        for cx in range(NC):
            if o or cx:
                src = dp_dev(o, cx)["dp"]
                wait_recv(lossb.at[src], ls_s.at[o * 2 + cx], ls_r.at[src])
    loss = lossb[0]
    for k in range(1, 8):
        loss = loss + lossb[k]
    out_loss[...] = loss * (1.0 / (8 * TOK))

    @pl.when(jnp.logical_not(src_self))
    def _():
        wait_recv(fin_in, f_s.at[0], f_r)

    both = fin_in[...].astype(F32)
    out_hidden[...] = jnp.where(vo % 2 == 0, both[:, :64], both[:, 64:]).astype(BF16)

    for copy in waits:
        copy.wait_send()

    @pl.loop(0, NQ)
    def _(q):
        sib_copy(q).wait_send()
        opp_copy(q).wait_send()
        nb_copy(q, 1).wait_send()
        nb_copy(q, 3).wait_send()

    for r, copy in zsends:
        @pl.when(r != 0)
        def _():
            copy.wait_send()

    @pl.when(sends_final)
    def _():
        for h in range(2):
            @pl.when(jnp.logical_not(dest_self[h]))
            def _():
                rc(fin, fin_in, f_s.at[h], f_r, {"dp": fin_block, "vocab": dest_v[h]}).wait_send()

    @pl.loop(0, nh)
    def _(n):
        head_copy(n).wait()


def per_device(hidden, head_weight, teacher_ids, teacher_logits):
    vm = pltpu.VMEM
    dma = pltpu.SemaphoreType.DMA
    scratch = [
        vm((VOCAB, FEAT), BF16),
        vm((NY, NC, TOK, FEAT), BF16),
        vm((NQ, NY, TOK, QC), F32),
        vm((NQ, NY, TOK, QC), F32),
        vm((NQ, NY, TOK, QC), F32),
        vm((NQ, TOK, QC), jnp.int16),
        vm((NQ, 2, TOK, QC), jnp.int16),
        vm((NQ, TOK, QC), jnp.int16),
        vm((NQ, 2, TOK, QC), jnp.int16),
        vm((TOK, K), F32),
        vm((TOK, NHI, 128), F32),
        vm((NHI, TOK, 128), F32),
        vm((NHI, TOK, 128), F32),
        vm((NX, 1, 128), F32),
        vm((NZ, 1, 128), F32),
        vm((8, 1, 128), F32),
        vm((NY, NC, TOK, VOCAB), BF16),
        vm((NY, NX, 2 * TOK, 128), F32),
        vm((NY, NX, 2 * TOK, 128), BF16),
        vm((NY, NX - 1, 2 * TOK, 128), BF16),
        vm((NY, NC, TOK, 128), BF16),
        vm((NZ, TOK, 128), BF16),
        vm((TOK, 128), BF16),
        vm((TOK, 128), BF16),
        vm((VOCAB, FEAT), BF16),
        dma((NQ,)), dma, dma((NY, NC)), dma((NY, NC)), dma((NQ,)), dma((NQ,)), dma((3, NQ)), dma((3, NQ)),
        dma((NX,)), dma((NX,)), dma((NZ,)), dma((NZ,)), dma((8,)), dma((8,)), dma((13,)), dma((13,)),
        dma((NY, NX - 1)), dma((NY, NX - 1)), dma((NY, NC)), dma((NZ,)), dma((2,)), dma, dma((VOCAB // 256,)),
    ]
    anys = pl.BlockSpec(memory_space=pl.ANY)
    vmem = pl.BlockSpec(memory_space=pltpu.VMEM)
    hidden_grad, head_grad, loss = pl.pallas_call(
        kernel,
        out_shape=(
            jax.ShapeDtypeStruct((TOK, D // 64), BF16),
            jax.ShapeDtypeStruct((VOCAB, FEAT), BF16),
            jax.ShapeDtypeStruct((1, 128), F32),
        ),
        in_specs=[anys, anys, vmem, vmem],
        out_specs=(vmem, anys, vmem),
        scratch_shapes=scratch,
        compiler_params=pltpu.CompilerParams(
            collective_id=0, has_side_effects=True, vmem_limit_bytes=40 * 1024 * 1024
        ),
    )(hidden, head_weight, teacher_ids, teacher_logits)
    return hidden_grad, head_grad, loss[0, 0]


def solution(mesh):
    in_specs = (P("dp", None), P("vocab", "dp"), P("dp", None), P("dp", None))
    out_specs = (P("dp", "vocab"), P("vocab", "dp"), P())
    return jax.shard_map(
        per_device, mesh=mesh, in_specs=in_specs, out_specs=out_specs, check_vma=False
    )
```

time: 989 us -> 91.5 us (0.09)
  the two profiles are of different devices: /device:TPU:16 before, /device:TPU:18 now
where the time goes in v1:
time: 91.5 us; the launch traced here: 91.2 us
  Pallas kernels  83.3 us (91%)
  local copies, waits for them, and re-layouts  6.1 us (7%)
  between operations  1.82 us (2%)
    pallas_call x1, Pallas kernels, per_device(): pl.pallas_call(kernel, out_shape=(jax.ShapeDtypeStruct((TOK, D // 64), BF...  83.3 us
    unnamed x10, local copies, waits for them, and re-layouts  6.1 us

profile of v1, /device:TPU:18, one launch (start us, length us, event | category | flops | bytes accessed | tf_op | source)
XLA Modules:
  0.0 91.2 jit_solution(8582251748987649373)
XLA Ops:
  0.6 0.0 copy-start
  0.6 1.6 %copy-done = bf16[2048,512]{1,0:T(8,128)(2,1)S(1)} copy-done((bf16[2048,512]{1,0:T(8,128)(2,1)S(1)}, bf16[2048,512]{1,0:T(8,128)(2,1)}, u32[]{:S(2)}) %copy-start) | copy-done | bytes 2097176
  2.2 0.0 copy-start.1
  2.2 1.0 %copy-done.1 = bf16[48,4096]{1,0:T(8,128)(2,1)S(1)} copy-done((bf16[48,4096]{1,0:T(8,128)(2,1)S(1)}, bf16[48,4096]{1,0:T(8,128)(2,1)}, u32[]{:S(2)}) %copy-start.1) | copy-done | bytes 393240
  3.2 0.0 copy-start.2
  3.2 0.8 copy-done.2
  4.0 0.0 copy-start.3
  4.0 0.8 copy-done.3
  4.8 83.3 %shard_map.67 = (bf16[48,64]{1,0:T(8,128)(2,1)S(1)}, bf16[2048,512]{1,0:T(8,128)(2,1)S(1)}, f32[1,128]{1,0:T(1,128)S(1)}) custom-call(bf16[48,4096]{1,0:T(8,128)(2,1)S(1)} %copy-done.1, bf16[2048,512]{1,0:T(8,128)(2,1)S(1)} %copy-done, s32[48,256]{1,0:T(8,128)S(1)} %copy-done.2, f32[48,256]{1,0:T(8,128)S(1)} %copy-done.3), custom_call_target="tpu_custom_call" | custom-call | tf_op jit(solution)/shard_map/pallas_call | solution.py:454
  88.1 0.6 copy.10
  88.7 1.3 %copy.11 = bf16[2048,512]{1,0:T(8,128)(2,1)} copy(bf16[2048,512]{1,0:T(8,128)(2,1)S(1)} %get-tuple-element.13) | data formatting | bytes 4194304
Async XLA Ops:
  0.6 1.6 %copy-start = (bf16[2048,512]{1,0:T(8,128)(2,1)S(1)}, bf16[2048,512]{1,0:T(8,128)(2,1)}, u32[]{:S(2)}) copy-start(bf16[2048,512]{1,0:T(8,128)(2,1)} %weight.1) | copy-start | bytes 6291460
  2.2 1.0 %copy-start.1 = (bf16[48,4096]{1,0:T(8,128)(2,1)S(1)}, bf16[48,4096]{1,0:T(8,128)(2,1)}, u32[]{:S(2)}) copy-start(bf16[48,4096]{1,0:T(8,128)(2,1)} %hidden.1) | copy-start | bytes 1179652
  3.2 0.8 copy-start.2
  4.0 0.8 copy-start.3

commit v2 on v1

v2 whole, which is shorter than its diff:
```python
import jax
import jax.numpy as jnp
from jax import lax
from jax.experimental import pallas as pl
from jax.experimental.pallas import tpu as pltpu
from jax.sharding import PartitionSpec as P

MESH = pl.DeviceIdType.MESH
F32 = jnp.float32
BF16 = jnp.bfloat16
soft_cap = 30.0

NY, NC, NX, NZ = 4, 2, 4, 16
TOK, D, K = 48, 4096, 256
FEAT = D // 8
VOCAB = 131072 // 64
NQ = 4
QC = VOCAB // NQ
NHI = VOCAB // 128
BEND = 48.0
LEVELS = 32767.0


def encode(x):
    return jnp.round(x * (LEVELS / (jnp.abs(x) + BEND))).astype(jnp.int32).astype(jnp.int16)


def decode(q):
    u = q.astype(jnp.int32).astype(F32)
    return u * (BEND / (LEVELS - jnp.abs(u)))


def mm(a, b, ca, cb):
    return lax.dot_general(a, b, (((ca,), (cb,)), ((), ())), preferred_element_type=F32)


def kernel(
    hidden, weight, ids_in, logits_in, out_hidden, out_head, out_loss,
    ids, logits, wv, hv, psib, pown, srecv, enc_opp, enc_nb, in_opp, in_nb,
    prob, tgt, es, om, psx, psz, lossb, gv, gt, xs, xr, ys, yr, zr, fin, fin_in,
    id_sem, w_sem, own_sem, hs_sem, hr_sem, ss_sem, sr_sem, rs_s, rs_r,
    px_s, px_r, pz_s, pz_r, ls_s, ls_r, ag_s, ag_r, x_s, x_r, y_s, y_r, z_s, z_r, f_s, f_r, hq_s, hq_r, hx_s, hx_r, near2, near4,
):
    me = lax.axis_index("dp")
    vo = lax.axis_index("vocab")
    y, c = me // 2, me % 2
    z, x = vo // NX, vo % NX

    def dp_dev(o, cx):
        return {"dp": ((y + o) % NY) * 2 + (c + cx) % 2, "vocab": vo}

    def x_dev(r):
        return {"dp": me, "vocab": z * NX + (x + r) % NX}

    def z_dev(zz):
        return {"dp": me, "vocab": zz * NX + x}

    def rc(src, dst, ssem, rsem, dev):
        return pltpu.make_async_remote_copy(
            src_ref=src, dst_ref=dst, send_sem=ssem, recv_sem=rsem, device_id=dev, device_id_type=MESH
        )

    waits = []

    def send(src, dst, ssem, rsem, dev):
        copy = rc(src, dst, ssem, rsem, dev)
        copy.start()
        waits.append(copy)

    def wait_recv(dst, ssem, rsem):
        rc(dst, dst, ssem, rsem, dp_dev(0, 1)).wait_recv()

    collects = z % 2 == c

    wcopies = []
    for q in range(NQ):
        rows = pl.ds(q * QC, QC)
        wcopies.append(pltpu.make_async_copy(weight.at[rows], wv.at[rows], w_sem.at[q]))
    own_h = pltpu.make_async_copy(hidden.at[:, pl.ds(pl.multiple_of(me * FEAT, FEAT), FEAT)], hv.at[0, 0], own_sem)
    own_h.start()
    id_copies = [
        pltpu.make_async_copy(ids_in, ids, id_sem.at[0]), pltpu.make_async_copy(logits_in, logits, id_sem.at[1])
    ]
    for w in id_copies + wcopies:
        w.start()

    barrier = pltpu.get_barrier_semaphore()

    def greet(dev):
        pl.semaphore_signal(barrier, inc=1, device_id=dev, device_id_type=MESH)

    for o in range(NY):
        for cx in range(NC):
            if o or cx:
                greet(dp_dev(o, cx))
    for r in range(1, NX):
        greet(x_dev(r))
    for r in (1, 2, NZ - 2, NZ - 1):
        greet(z_dev((z + r) % NZ))

    pl.semaphore_wait(barrier, 7 + (NX - 1) + 4)

    def tell(sem, step):
        for r in (step, NZ - step):
            pl.semaphore_signal(sem, inc=1, device_id=z_dev((z + r) % NZ), device_id_type=MESH)


    quarter = pl.ds(pl.multiple_of(x * 128, 128), 128)
    for cx in range(NC):
        dev = dp_dev(2, cx)
        cols = pl.ds(pl.multiple_of(dev["dp"] * FEAT + x * 128, 128), 128)
        send(hidden.at[:, cols], hv.at[2, cx, :, quarter], hq_s.at[cx], hq_r.at[cx], dev)
    for o, cx in ((1, 0), (3, 0), (1, 1), (3, 1), (0, 1)):
        dev = dp_dev(o, cx)
        back = (-o) % NY
        cols = pl.ds(pl.multiple_of(dev["dp"] * FEAT, FEAT), FEAT)
        send(hidden.at[:, cols], hv.at[back, cx], hs_sem.at[o, cx], hr_sem.at[back, cx], dev)
    tell(near2, 2)

    for w in id_copies:
        w.wait()
    lg = logits[...]
    logp = lg - jnp.log(jnp.sum(jnp.exp(lg), axis=1, keepdims=True))
    pr = jnp.exp(logp)
    prob[...] = pr
    entropy = jnp.sum(pr * logp, axis=1, keepdims=True)

    first = vo * VOCAB
    rows16 = lax.broadcasted_iota(jnp.int32, (NHI, K), 0)
    rows128 = lax.broadcasted_iota(jnp.int32, (128, K), 0)

    def target_tokens(n):
        for k in range(4):
            t = n * 4 + k
            place = ids[pl.ds(t, 1), :] - first
            p = prob[pl.ds(t, 1), :]
            a = jnp.where((place >> 7) == rows16, p, 0.0)
            a1 = a.astype(BF16)
            rest = a - a1.astype(F32)
            a2 = rest.astype(BF16)
            a3 = (rest - a2.astype(F32)).astype(BF16)
            b = jnp.where((place & 127) == rows128, 1.0, 0.0).astype(BF16)
            both = mm(jnp.concatenate([a1, a2, a3], axis=0), b, 1, 1)
            tgt[t] = both[0:NHI] + both[NHI:2 * NHI] + both[2 * NHI:3 * NHI]

    pl.loop(0, 5)(target_tokens)
    for cx in range(NC):
        part = hv.at[2, cx, :, quarter]
        wait_recv(part, hq_s.at[cx], hq_r.at[cx])
        for r in range(1, NX):
            send(part, part, hx_s.at[cx, r], hx_r.at[cx, (-r) % NX], x_dev(r))
    pl.loop(5, TOK // 4)(target_tokens)
    pl.semaphore_wait(near2, 2)
    tell(near4, 4)
    for q in range(NQ):
        wcopies[q].wait()
    def hidden_far(cx):
        for r in range(1, NX):
            part = hv.at[2, cx, :, pl.ds(pl.multiple_of(((x + r) % NX) * 128, 128), 128)]
            wait_recv(part, hx_s.at[cx, r], hx_r.at[cx, r])

    for o in (0, 1, 3):
        wait_recv(hv.at[o, 1], hs_sem.at[o, 1], hr_sem.at[o, 1])
    hidden_far(1)

    def q_of(s):
        return (s % 2) * 2 + s // 2

    def sib_copy(q):
        return rc(psib.at[q], srecv.at[q], ss_sem.at[q], sr_sem.at[q], dp_dev(0, 1))

    own_h.wait()
    for o in (1, 3):
        wait_recv(hv.at[o, 0], hs_sem.at[o, 0], hr_sem.at[o, 0])
    hidden_far(0)

    def way(q):
        return 1 + 2 * (q // 2)

    def opp_copy(q):
        return rc(enc_opp.at[q], in_opp.at[q], rs_s.at[0, q], rs_r.at[0, q], dp_dev(way(q), 0))

    def nb_copy(q, o):
        slot, back = o // 2, 1 - o // 2
        return rc(enc_nb.at[q, slot], in_nb.at[q, back], rs_s.at[1 + slot, q], rs_r.at[1 + back, q], dp_dev(o, 0))

    def logits_part(q, cx):
        hb = hv[:, cx].reshape(NY * TOK, FEAT)
        part = mm(hb, wv[pl.ds(pl.multiple_of(q * QC, QC), QC), :], 1, 1)
        return part.reshape(NY, TOK, QC)

    @pl.loop(0, NQ + 3)
    def _(s):
        @pl.when(s < NQ)
        def _():
            q = q_of(s)
            psib[q] = logits_part(q, 1)
            sib_copy(q).start()

        @pl.when(jnp.logical_and(s > 0, s <= NQ))
        def _():
            q = q_of(s - 1)
            pown[q] = logits_part(q, 0)
            wait_recv(srecv.at[q], ss_sem.at[q], sr_sem.at[q])
            enc_opp[q] = encode(pown[q, 2] + srecv[q, 2])
            opp_copy(q).start()
            other = 4 - way(q)
            enc_nb[q, other // 2] = encode(pown[q, other] + srecv[q, other])
            nb_copy(q, other).start()

        @pl.when(s > 2)
        def _():
            q = q_of(s - 3)
            wait_recv(in_opp.at[q], rs_s.at[0, q], rs_r.at[0, q])
            o = way(q)
            enc_nb[q, o // 2] = encode(pown[q, o] + srecv[q, o] + decode(in_opp[q]))
            nb_copy(q, o).start()

    tot = jnp.zeros((TOK, 128), F32)
    crs = jnp.zeros((TOK, 128), F32)
    for s in range(NQ):
        q = q_of(s)
        for slot in range(2):
            wait_recv(in_nb.at[q, slot], rs_s.at[1 + slot, q], rs_r.at[1 + slot, q])
        for k in range(QC // 128):
            cols = slice(k * 128, (k + 1) * 128)
            hi = q * (QC // 128) + k
            raw = (
                pown[q, 0, :, cols] + srecv[q, 0, :, cols]
                + decode(in_nb[q, 0, :, cols]) + decode(in_nb[q, 1, :, cols])
            )
            squash = jnp.tanh(raw * (1.0 / soft_cap))
            student = soft_cap * squash
            expo = jnp.exp(student)
            es[hi] = expo
            om[hi] = 1.0 - squash * squash
            tot = tot + expo
            crs = crs + tgt[:, hi, :] * student

    lane = lax.broadcasted_iota(jnp.int32, (TOK, 128), 1)
    row = lax.broadcasted_iota(jnp.int32, (TOK, 128), 0)
    mine = jnp.where(lane == row, jnp.sum(tot, axis=1, keepdims=True), 0.0) + jnp.where(
        lane == row + 64, jnp.sum(crs, axis=1, keepdims=True), 0.0
    )
    psx[x] = jnp.sum(mine, axis=0, keepdims=True)
    for r in range(1, NX):
        send(psx.at[x], psx.at[x], px_s.at[r], px_r.at[x], x_dev(r))
    for r in range(1, NX):
        src = (x + r) % NX
        wait_recv(psx.at[src], px_s.at[r], px_r.at[src])
    pl.semaphore_wait(near4, 2)
    psz[z] = psx[0] + psx[1] + psx[2] + psx[3]
    for r in range(1, NZ):
        send(psz.at[z], psz.at[z], pz_s.at[r], pz_r.at[z], z_dev((z + r) % NZ))
    for r in range(1, NZ):
        src = (z + r) % NZ
        wait_recv(psz.at[src], pz_s.at[r], pz_r.at[src])
    sums = psz[0]
    for k in range(1, NZ):
        sums = sums + psz[k]
    sums = jnp.broadcast_to(sums, (TOK, 128))
    total = jnp.sum(jnp.where(lane == row, sums, 0.0), axis=1, keepdims=True)
    cross = jnp.sum(jnp.where(lane == row + 64, sums, 0.0), axis=1, keepdims=True)
    inv = 1.0 / total
    for hi in range(NHI):
        g = (es[hi] * inv - tgt[:, hi, :]) * om[hi]
        gv[0, 0, :, hi * 128:(hi + 1) * 128] = g.astype(BF16)

    half = [pl.ds(0, VOCAB // 2), pl.ds(VOCAB // 2, VOCAB // 2)]

    def pass_on(n, o, h, do, dcx):
        back = (o - do) % NY
        src = gv.at[o, 0] if h is None else gv.at[o, 0, :, half[h]]
        dst = gv.at[back, dcx] if h is None else gv.at[back, dcx, :, half[h]]
        send(src, dst, ag_s.at[n], ag_r.at[n], dp_dev(do, dcx))

    def arrived(n, o, cx, h):
        dst = gv.at[o, cx] if h is None else gv.at[o, cx, :, half[h]]
        wait_recv(dst, ag_s.at[n], ag_r.at[n])

    pass_on(0, 0, 0, 1, 0)
    pass_on(1, 0, 1, 3, 0)
    pass_on(2, 0, None, 0, 1)
    pass_on(3, 0, 1, 1, 0)
    pass_on(4, 0, 0, 3, 0)

    token_loss = entropy - cross + jnp.log(total)
    lossb[me] = jnp.broadcast_to(jnp.sum(token_loss, axis=0, keepdims=True), (1, 128))
    for o in range(NY):
        for cx in range(NC):
            if o or cx:
                dev = dp_dev(o, cx)
                send(lossb.at[me], lossb.at[me], ls_s.at[o * 2 + cx], ls_r.at[me], dev)

    def terms(o):
        ga = gv[o].reshape(2 * TOK, VOCAB)
        part = [mm(ga, wv[:, n * 256:(n + 1) * 256], 1, 0) for n in range(2)]
        for m in range(NX):
            cols = slice(m * 64, (m + 1) * 64)
            piece = jnp.concatenate([part[0][:, cols], part[1][:, cols]], axis=1)
            gt[o, m] = piece
            xs[o, m] = piece.astype(BF16)
        for r in range(1, NX):
            there = (x + r) % NX
            send(xs.at[o, there], xr.at[o, (-r) % NX - 1], x_s.at[o, r - 1], x_r.at[o, (-r) % NX - 1], x_dev(r))

    def to_y(o):
        for r in range(NX - 1):
            wait_recv(xr.at[o, r], x_s.at[o, r], x_r.at[o, r])
        val = gt[o, x]
        for r in range(NX - 1):
            val = val + xr[o, r].astype(F32)
        for cx in range(NC):
            mine = val[cx * TOK:(cx + 1) * TOK].astype(BF16)
            if o or cx:
                ys[o, cx] = mine
                back = (-o) % NY
                send(ys.at[o, cx], yr.at[back, cx], y_s.at[o, cx], y_r.at[back, cx], dp_dev(o, cx))
            else:
                yr[0, 0] = mine

    zsends = []

    def to_z(o):
        for cx in range(NC):
            if o or cx:
                wait_recv(yr.at[o, cx], y_s.at[o, cx], y_r.at[o, cx])
            zd = 2 * dp_dev(o, cx)["dp"] + c
            r = (z - zd + NZ) % NZ
            copy = rc(yr.at[o, cx], zr.at[r], z_s.at[o, cx], z_r.at[r], z_dev(zd))

            @pl.when(r != 0)
            def _():
                copy.start()

            zsends.append((r, copy))

            @pl.when(r == 0)
            def _():
                zr[0] = yr[o, cx]

    arrived(0, 3, 0, 0)
    pass_on(5, 3, 0, 1, 0)
    pass_on(7, 3, 0, 0, 1)
    arrived(1, 1, 0, 1)
    pass_on(6, 1, 1, 3, 0)
    pass_on(8, 1, 1, 0, 1)
    arrived(2, 0, 1, None)
    terms(0)
    arrived(3, 3, 0, 1)
    pass_on(9, 3, 1, 0, 1)
    arrived(4, 1, 0, 0)
    pass_on(10, 1, 0, 0, 1)
    arrived(8, 1, 1, 1)
    arrived(10, 1, 1, 0)
    terms(1)
    arrived(7, 3, 1, 0)
    arrived(9, 3, 1, 1)
    terms(3)
    to_y(0)
    arrived(5, 2, 0, 0)
    pass_on(11, 2, 0, 0, 1)
    arrived(6, 2, 0, 1)
    pass_on(12, 2, 1, 0, 1)
    to_z(0)
    arrived(11, 2, 1, 0)
    arrived(12, 2, 1, 1)
    terms(2)
    to_y(1)
    to_y(3)

    HB = 256

    def head_part(low, high):
        @pl.loop(low, high)
        def _(n):
            rows = pl.ds(pl.multiple_of(n * HB, HB), HB)
            ga = gv[:, :, :, rows].reshape(8 * TOK, HB)
            hb = hv[...].reshape(8 * TOK, FEAT)
            out_head[rows, :] = mm(ga, hb, 0, 0).astype(BF16)

    nh = VOCAB // HB
    head_part(0, 2)
    to_y(2)
    to_z(3)
    to_z(1)
    head_part(2, 4)
    to_z(2)
    head_part(4, nh)
    for o in range(NY):
        for cx in range(NC):
            if o or cx:
                src = dp_dev(o, cx)["dp"]
                wait_recv(lossb.at[src], ls_s.at[o * 2 + cx], ls_r.at[src])
    loss = lossb[0]
    for k in range(1, 8):
        loss = loss + lossb[k]
    out_loss[...] = loss * (1.0 / (8 * TOK))


    def pair_copy():
        return rc(fin, fin_in, f_s, f_r, z_dev(z + 1 - 2 * (z % 2)))

    @pl.when(collects)
    def _():
        acc = zr[0].astype(F32)
        for r in range(1, NZ):
            wait_recv(zr.at[r], f_s, z_r.at[r])
            acc = acc + zr[r].astype(F32)
        fin[...] = acc.astype(BF16)
        pair_copy().start()
        fin_in[...] = fin[...]


    @pl.when(jnp.logical_not(collects))
    def _():
        wait_recv(fin_in, f_s, f_r)

    both = fin_in[...].astype(F32)
    out_hidden[...] = jnp.where(z % 2 == 0, both[:, :64], both[:, 64:]).astype(BF16)

    for copy in waits:
        copy.wait_send()

    @pl.loop(0, NQ)
    def _(q):
        sib_copy(q).wait_send()
        opp_copy(q).wait_send()
        nb_copy(q, 1).wait_send()
        nb_copy(q, 3).wait_send()

    for r, copy in zsends:
        @pl.when(r != 0)
        def _():
            copy.wait_send()

    @pl.when(collects)
    def _():
        pair_copy().wait_send()


def per_device(hidden, head_weight, teacher_ids, teacher_logits):
    vm = pltpu.VMEM
    dma = pltpu.SemaphoreType.DMA
    scratch = [
        vm((TOK, K), jnp.int32),
        vm((TOK, K), F32),
        vm((VOCAB, FEAT), BF16),
        vm((NY, NC, TOK, FEAT), BF16),
        vm((NQ, NY, TOK, QC), F32),
        vm((NQ, NY, TOK, QC), F32),
        vm((NQ, NY, TOK, QC), F32),
        vm((NQ, TOK, QC), jnp.int16),
        vm((NQ, 2, TOK, QC), jnp.int16),
        vm((NQ, TOK, QC), jnp.int16),
        vm((NQ, 2, TOK, QC), jnp.int16),
        vm((TOK, K), F32),
        vm((TOK, NHI, 128), F32),
        vm((NHI, TOK, 128), F32),
        vm((NHI, TOK, 128), F32),
        vm((NX, 1, 128), F32),
        vm((NZ, 1, 128), F32),
        vm((8, 1, 128), F32),
        vm((NY, NC, TOK, VOCAB), BF16),
        vm((NY, NX, 2 * TOK, 128), F32),
        vm((NY, NX, 2 * TOK, 128), BF16),
        vm((NY, NX - 1, 2 * TOK, 128), BF16),
        vm((NY, NC, TOK, 128), BF16),
        vm((NY, NC, TOK, 128), BF16),
        vm((NZ, TOK, 128), BF16),
        vm((TOK, 128), BF16),
        vm((TOK, 128), BF16),
        dma((2,)), dma((NQ,)), dma, dma((NY, NC)), dma((NY, NC)), dma((NQ,)), dma((NQ,)), dma((3, NQ)), dma((3, NQ)),
        dma((NX,)), dma((NX,)), dma((NZ,)), dma((NZ,)), dma((8,)), dma((8,)), dma((13,)), dma((13,)),
        dma((NY, NX - 1)), dma((NY, NX - 1)), dma((NY, NC)), dma((NY, NC)), dma((NY, NC)), dma((NZ,)), dma, dma,
        dma((NC,)), dma((NC,)), dma((NC, NX)), dma((NC, NX)),
        pltpu.SemaphoreType.REGULAR, pltpu.SemaphoreType.REGULAR,
    ]
    hbm = pl.BlockSpec(memory_space=pltpu.HBM)
    vmem = pl.BlockSpec(memory_space=pltpu.VMEM)
    hidden_grad, head_grad, loss = pl.pallas_call(
        kernel,
        out_shape=(
            pltpu.VMEM((TOK, D // 64), BF16),
            pltpu.VMEM((VOCAB, FEAT), BF16),
            pltpu.VMEM((1, 128), F32),
        ),
        in_specs=[hbm, hbm, hbm, hbm],
        out_specs=(vmem, vmem, vmem),
        scratch_shapes=scratch,
        compiler_params=pltpu.CompilerParams(
            collective_id=0, has_side_effects=True, vmem_limit_bytes=56 * 1024 * 1024
        ),
    )(hidden, head_weight, teacher_ids, teacher_logits)
    return hidden_grad, head_grad, loss[0, 0]


def solution(mesh):
    in_specs = (P("dp", None), P("vocab", "dp"), P("dp", None), P("dp", None))
    out_specs = (P("dp", "vocab"), P("vocab", "dp"), P())
    return jax.shard_map(
        per_device, mesh=mesh, in_specs=in_specs, out_specs=out_specs, check_vma=False
    )
```

time: 91.5 us -> 75.6 us (0.83)
  the two profiles are of different devices: /device:TPU:18 before, /device:TPU:48 now
where the time goes in v2:
time: 75.6 us; the launch traced here: 75.5 us
  Pallas kernels  71.7 us (95%)
  local copies, waits for them, and re-layouts  1.92 us (3%)
  between operations  1.8 us (2%)
    pallas_call x1, Pallas kernels, per_device(): pl.pallas_call(kernel, out_shape=(pltpu.VMEM((TOK, D // 64), BF16), pltpu...  71.7 us
    unnamed x2, local copies, waits for them, and re-layouts  1.92 us

profile of v2, /device:TPU:48, one launch (start us, length us, event | category | flops | bytes accessed | tf_op | source)
XLA Modules:
  0.0 75.5 jit_solution(9908509334475208278)
XLA Ops:
  0.6 71.7 %shard_map.67 = (bf16[48,64]{1,0:T(8,128)(2,1)S(1)}, bf16[2048,512]{1,0:T(8,128)(2,1)S(1)}, f32[1,128]{1,0:T(1,128)S(1)}) custom-call(bf16[48,4096]{1,0:T(8,128)(2,1)} %hidden.1, bf16[2048,512]{1,0:T(8,128)(2,1)} %weight.1, s32[48,256]{1,0:T(8,128)} %ids_in.1, f32[48,256]{1,0:T(8,128)} %logits_in.1), custom_call_target="tpu_custom_call" | custom-call | tf_op jit(solution)/shard_map/pallas_call | solution.py:481
  72.4 0.6 copy.10
  73.0 1.3 %copy.11 = bf16[2048,512]{1,0:T(8,128)(2,1)} copy(bf16[2048,512]{1,0:T(8,128)(2,1)S(1)} %get-tuple-element.10) | data formatting | bytes 4194304

commit v3 on v2

v3 whole, which is shorter than its diff:
```python
import jax
import jax.numpy as jnp
from jax import lax
from jax.experimental import pallas as pl
from jax.experimental.pallas import tpu as pltpu
from jax.sharding import PartitionSpec as P

MESH = pl.DeviceIdType.MESH
F32 = jnp.float32
BF16 = jnp.bfloat16
soft_cap = 30.0

NY, NC, NX, NZ = 4, 2, 4, 16
TOK, D, K = 48, 4096, 256
FEAT = D // 8
VOCAB = 131072 // 64
NQ = 4
QC = VOCAB // NQ
NHI = VOCAB // 128
BEND = 48.0
LEVELS = 32767.0


def encode(x):
    return jnp.round(x * (LEVELS / (jnp.abs(x) + BEND))).astype(jnp.int32).astype(jnp.int16)


def decode(q):
    u = q.astype(jnp.int32).astype(F32)
    return u * (BEND / (LEVELS - jnp.abs(u)))


def mm(a, b, ca, cb):
    return lax.dot_general(a, b, (((ca,), (cb,)), ((), ())), preferred_element_type=F32)


def kernel(
    hidden, weight, ids_in, logits_in, out_hidden, out_head, out_loss,
    ids, logits, wv, hv, psib, pown, srecv, enc_opp, enc_nb, in_opp, in_nb,
    prob, tgt, es, om, psx, psz, lossb, gv, gt, xs, xr, ys, yr, zr, head, hidden_v, loss_v,
    id_sem, w_sem, own_sem, hs_sem, hr_sem, ss_sem, sr_sem, rs_s, rs_opp, rs_nb,
    px_s, px_r, pz_s, pz_r, ls_s, ls_r, ag_s, ag_r, x_s, x_r, y_s, y_r, z_s, z_r, head_sem, out_sem, near2, near4,
):
    me = lax.axis_index("dp")
    vo = lax.axis_index("vocab")
    y, c = me // 2, me % 2
    z, x = vo // NX, vo % NX

    def dp_dev(o, cx):
        return {"dp": ((y + o) % NY) * 2 + (c + cx) % 2, "vocab": vo}

    def x_dev(r):
        return {"dp": me, "vocab": z * NX + (x + r) % NX}

    def z_dev(zz):
        return {"dp": me, "vocab": zz * NX + x}

    def rc(src, dst, ssem, rsem, dev):
        return pltpu.make_async_remote_copy(
            src_ref=src, dst_ref=dst, send_sem=ssem, recv_sem=rsem, device_id=dev, device_id_type=MESH
        )


    def came(ref, sem):
        rc(ref, ref, hs_sem.at[0], sem, dp_dev(0, 1)).wait_recv()

    def gone(ref, sem):
        rc(ref, ref, sem, hr_sem.at[0], dp_dev(0, 1)).wait_send()

    w_copy = pltpu.make_async_copy(weight, wv, w_sem)
    own_h = pltpu.make_async_copy(hidden.at[:, pl.ds(pl.multiple_of(me * FEAT, FEAT), FEAT)], hv.at[0, 0], own_sem)
    own_h.start()
    id_copies = [
        pltpu.make_async_copy(ids_in, ids, id_sem.at[0]), pltpu.make_async_copy(logits_in, logits, id_sem.at[1])
    ]
    for w in id_copies:
        w.start()
    w_copy.start()

    barrier = pltpu.get_barrier_semaphore()

    def greet(dev):
        pl.semaphore_signal(barrier, inc=1, device_id=dev, device_id_type=MESH)

    for o in range(NY):
        for cx in range(NC):
            if o or cx:
                greet(dp_dev(o, cx))
    for r in range(1, NX):
        greet(x_dev(r))
    for r in (1, 2, NZ - 2, NZ - 1):
        greet(z_dev((z + r) % NZ))

    pl.semaphore_wait(barrier, 7 + (NX - 1) + 4)

    def tell(sem, step):
        for r in (step, NZ - step):
            pl.semaphore_signal(sem, inc=1, device_id=z_dev((z + r) % NZ), device_id_type=MESH)


    def hidden_copy(o, cx):
        dev = dp_dev(o, cx)
        back = (-o) % NY
        cols = pl.ds(pl.multiple_of(dev["dp"] * FEAT, FEAT), FEAT)
        n = (0, 1, 2, 1)[o]
        return rc(hidden.at[:, cols], hv.at[back, cx], hs_sem.at[n], hr_sem.at[n], dev)

    for o, cx in ((2, 0), (2, 1), (0, 1)):
        hidden_copy(o, cx).start()
    tell(near2, 2)

    for w in id_copies:
        w.wait()
    lg = logits[...]
    logp = lg - jnp.log(jnp.sum(jnp.exp(lg), axis=1, keepdims=True))
    pr = jnp.exp(logp)
    prob[...] = pr
    entropy = jnp.sum(pr * logp, axis=1, keepdims=True)

    first = vo * VOCAB
    rows16 = lax.broadcasted_iota(jnp.int32, (NHI, K), 0)
    rows128 = lax.broadcasted_iota(jnp.int32, (128, K), 0)

    def target_tokens(n):
        for k in range(4):
            t = n * 4 + k
            place = ids[pl.ds(t, 1), :] - first
            p = prob[pl.ds(t, 1), :]
            a = jnp.where((place >> 7) == rows16, p, 0.0)
            a1 = a.astype(BF16)
            rest = a - a1.astype(F32)
            a2 = rest.astype(BF16)
            a3 = (rest - a2.astype(F32)).astype(BF16)
            b = jnp.where((place & 127) == rows128, 1.0, 0.0).astype(BF16)
            both = mm(jnp.concatenate([a1, a2, a3], axis=0), b, 1, 1)
            tgt[t] = both[0:NHI] + both[NHI:2 * NHI] + both[2 * NHI:3 * NHI]


    place_of = (0, 2, 1, 3)

    def partial_logits(q, offsets):
        hb = jnp.concatenate([hv[o].reshape(NC * TOK, FEAT) for o in offsets], axis=0)
        part = mm(hb, wv[pl.ds(pl.multiple_of(q * QC, QC), QC), :], 1, 1)
        for n, o in enumerate(offsets):
            pown[q, place_of[o]] = part[2 * n * TOK:(2 * n + 1) * TOK]
            psib[q, place_of[o]] = part[(2 * n + 1) * TOK:(2 * n + 2) * TOK]

    def sib_copy(q, offsets):
        places = pl.ds(place_of[offsets[0]], len(offsets))
        n = 0 if offsets == (0,) else 1 + q + NQ * (len(offsets) - 1)
        return rc(psib.at[q, places], srecv.at[q, places], ss_sem, sr_sem.at[n], dp_dev(0, 1))

    def q_of(s):
        return (s % 2) * 2 + s // 2

    def way(q):
        return 1 + 2 * (q // 2)

    def opp_copy(q):
        return rc(enc_opp.at[q], in_opp.at[q], rs_s.at[0], rs_opp.at[q], dp_dev(way(q), 0))

    def nb_copy(q, o):
        slot, back = o // 2, 1 - o // 2
        return rc(enc_nb.at[q, slot], in_nb.at[q, back], rs_s.at[1], rs_nb.at[q], dp_dev(o, 0))

    w_copy.wait()
    own_h.wait()
    came(hv.at[0, 1], hr_sem.at[0])

    @pl.loop(0, NQ)
    def _(q):
        partial_logits(q, (0,))
        sib_copy(q, (0,)).start()

    gone(hv.at[0], hs_sem.at[2])
    for o, cx in ((1, 0), (3, 0), (1, 1), (3, 1)):
        hidden_copy(o, cx).start()
    pl.loop(0, TOK // 4)(target_tokens)
    pl.semaphore_wait(near2, 2)
    tell(near4, 4)
    came(hv.at[2], hr_sem.at[2])

    @pl.loop(0, NQ + 1)
    def _(s):
        @pl.when(s < NQ)
        def _():
            q = q_of(s)
            partial_logits(q, (2,))
            sib_copy(q, (2,)).start()

        @pl.when(s > 0)
        def _():
            q = q_of(s - 1)
            sib_copy(q, (2,)).wait_recv()
            enc_opp[q] = encode(pown[q, 1] + srecv[q, 1])
            opp_copy(q).start()

    came(hv.at[pl.ds(0, 2)], hr_sem.at[1])

    @pl.loop(0, NQ + 2)
    def _(s):
        @pl.when(s < NQ)
        def _():
            q = q_of(s)
            partial_logits(q, (1, 3))
            sib_copy(q, (1, 3)).start()

        @pl.when(jnp.logical_and(s > 0, s <= NQ))
        def _():
            q = q_of(s - 1)
            sib_copy(q, (1, 3)).wait_recv()
            o = 4 - way(q)
            enc_nb[q, o // 2] = encode(pown[q, 2 + o // 2] + srecv[q, 2 + o // 2])
            nb_copy(q, o).start()

        @pl.when(s > 1)
        def _():
            q = q_of(s - 2)
            opp_copy(q).wait_recv()
            o = way(q)
            enc_nb[q, o // 2] = encode(pown[q, 2 + o // 2] + srecv[q, 2 + o // 2] + decode(in_opp[q]))
            nb_copy(q, o).start()

    tot = jnp.zeros((TOK, 128), F32)
    crs = jnp.zeros((TOK, 128), F32)
    came(srecv.at[:, 0], sr_sem.at[0])
    for s in range(NQ):
        q = q_of(s)
        came(in_nb.at[q], rs_nb.at[q])
        for k in range(QC // 128):
            cols = slice(k * 128, (k + 1) * 128)
            hi = q * (QC // 128) + k
            raw = (
                pown[q, 0, :, cols] + srecv[q, 0, :, cols]
                + decode(in_nb[q, 0, :, cols]) + decode(in_nb[q, 1, :, cols])
            )
            squash = jnp.tanh(raw * (1.0 / soft_cap))
            student = soft_cap * squash
            expo = jnp.exp(student)
            es[hi] = expo
            om[hi] = 1.0 - squash * squash
            tot = tot + expo
            crs = crs + tgt[:, hi, :] * student

    lane = lax.broadcasted_iota(jnp.int32, (TOK, 128), 1)
    row = lax.broadcasted_iota(jnp.int32, (TOK, 128), 0)
    mine = jnp.where(lane == row, jnp.sum(tot, axis=1, keepdims=True), 0.0) + jnp.where(
        lane == row + 64, jnp.sum(crs, axis=1, keepdims=True), 0.0
    )
    psx[x] = jnp.sum(mine, axis=0, keepdims=True)
    for r in range(1, NX):
        rc(psx.at[x], psx.at[x], px_s, px_r, x_dev(r)).start()
    came(psx.at[pl.ds(0, NX - 1)], px_r)
    pl.semaphore_wait(near4, 2)
    psz[z] = psx[0] + psx[1] + psx[2] + psx[3]
    for r in (8, 7, 9, 6, 10, 5, 11, 4, 12, 3, 13, 2, 14, 1, 15):
        rc(psz.at[z], psz.at[z], pz_s, pz_r, z_dev((z + r) % NZ)).start()
    came(psz.at[pl.ds(0, NZ - 1)], pz_r)
    sums = psz[0]
    for k in range(1, NZ):
        sums = sums + psz[k]
    sums = jnp.broadcast_to(sums, (TOK, 128))
    total = jnp.sum(jnp.where(lane == row, sums, 0.0), axis=1, keepdims=True)
    cross = jnp.sum(jnp.where(lane == row + 64, sums, 0.0), axis=1, keepdims=True)
    inv = 1.0 / total
    for hi in range(NHI):
        g = (es[hi] * inv - tgt[:, hi, :]) * om[hi]
        gv[0, 0, :, hi * 128:(hi + 1) * 128] = g.astype(BF16)

    half = [pl.ds(0, VOCAB // 2), pl.ds(VOCAB // 2, VOCAB // 2)]

    def pass_on(o, h, do, dcx, ssem, rsem):
        back = (o - do) % NY
        src = gv.at[o, 0] if h is None else gv.at[o, 0, :, half[h]]
        dst = gv.at[back, dcx] if h is None else gv.at[back, dcx, :, half[h]]
        rc(src, dst, ag_s.at[ssem], ag_r.at[rsem], dp_dev(do, dcx)).start()

    pass_on(0, 0, 1, 0, 0, 0)
    pass_on(0, 1, 3, 0, 0, 1)
    pass_on(0, None, 0, 1, 1, 2)

    token_loss = entropy - cross + jnp.log(total)
    lossb[me] = jnp.broadcast_to(jnp.sum(token_loss, axis=0, keepdims=True), (1, 128))
    for o in range(NY):
        for cx in range(NC):
            if o or cx:
                dev = dp_dev(o, cx)
                rc(lossb.at[me], lossb.at[me], ls_s, ls_r, dev).start()

    def terms(offsets):
        ga = jnp.concatenate([gv[o].reshape(NC * TOK, VOCAB) for o in offsets], axis=0)
        part = [mm(ga, wv[:, n * 256:(n + 1) * 256], 1, 0) for n in range(2)]
        for n, o in enumerate(offsets):
            rows = slice(n * NC * TOK, (n + 1) * NC * TOK)
            for m in range(NX):
                cols = slice(m * 64, (m + 1) * 64)
                piece = jnp.concatenate([part[0][rows, cols], part[1][rows, cols]], axis=1)
                gt[o, m] = piece
                xs[o, m] = piece.astype(BF16)
            for r in range(1, NX):
                there = (x + r) % NX
                rc(xs.at[o, there], xr.at[o, (-r) % NX - 1], x_s, x_r.at[o], x_dev(r)).start()

    def to_y(o):
        came(xr.at[o], x_r.at[o])
        val = gt[o, x]
        for r in range(NX - 1):
            val = val + xr[o, r].astype(F32)
        for cx in range(NC):
            top, low = val[cx * TOK:cx * TOK + 24], val[cx * TOK + 24:(cx + 1) * TOK]
            gap = jnp.zeros((8, 128), F32)
            mine = jnp.concatenate(
                [
                    jnp.concatenate([top[:, :64], low[:, :64]], axis=1), gap,
                    jnp.concatenate([top[:, 64:], low[:, 64:]], axis=1), gap,
                ],
                axis=0,
            ).astype(BF16)
            if o or cx:
                n = o * NC + cx
                ys[n] = mine
                back = (-o) % NY
                rc(ys.at[n], yr.at[back, cx], y_s, y_r.at[back], dp_dev(o, cx)).start()
            else:
                yr[0, 0] = mine

    def to_z(o):
        came(yr.at[o] if o else yr.at[0, 1], y_r.at[o])
        for cx in range(NC):
            for h in range(2):
                zd = 2 * dp_dev(o, cx)["dp"] + h
                r = (z - zd + NZ) % NZ
                part = yr.at[o, cx, pl.ds(32 * h, 32)]
                copy = rc(part, zr.at[r], z_s, z_r, z_dev(zd))
                here = r == 0

                @pl.when(jnp.logical_not(here))
                def _():
                    copy.start()

                @pl.when(here)
                def _():
                    zr[0] = yr[o, cx, 32 * h:32 * h + 32]

    gone(gv.at[0, 0], ag_s.at[0])
    pass_on(0, 1, 1, 0, 2, 3)
    pass_on(0, 0, 3, 0, 2, 3)
    came(gv.at[3, 0, :, half[0]], ag_r.at[0])
    pass_on(3, 0, 1, 0, 3, 4)
    pass_on(3, 0, 0, 1, 4, 6)
    came(gv.at[1, 0, :, half[1]], ag_r.at[1])
    pass_on(1, 1, 3, 0, 3, 5)
    pass_on(1, 1, 0, 1, 4, 6)
    came(gv.at[0, 1], ag_r.at[2])
    terms((0,))
    came(gv.at[0, 0], ag_r.at[3])
    pass_on(3, 1, 0, 1, 4, 6)
    pass_on(1, 0, 0, 1, 4, 6)
    came(gv.at[0], ag_r.at[6])
    terms((1, 3))
    for h in range(2):
        came(gv.at[2, 0, :, half[h]], ag_r.at[4 + h])
        pass_on(2, h, 0, 1, 5, 7)
    to_y(0)
    came(gv.at[2, 1], ag_r.at[7])
    terms((2,))
    to_z(0)
    to_y(1)
    to_y(3)

    HB = 256

    def head_copy(n):
        rows = pl.ds(pl.multiple_of(n * HB, HB), HB)
        return pltpu.make_async_copy(head.at[rows], out_head.at[rows], head_sem)

    def head_part(low, high):
        @pl.loop(low, high)
        def _(n):
            rows = pl.ds(pl.multiple_of(n * HB, HB), HB)
            ga = gv[:, :, :, rows].reshape(8 * TOK, HB)
            hb = hv[...].reshape(8 * TOK, FEAT)
            head[rows, :] = mm(ga, hb, 0, 0).astype(BF16)
            head_copy(n).start()

    nh = VOCAB // HB
    head_part(0, 2)
    to_y(2)
    to_z(3)
    to_z(1)
    head_part(2, 4)
    to_z(2)
    head_part(4, nh)
    came(lossb.at[pl.ds(0, 7)], ls_r)
    loss = lossb[0]
    for k in range(1, 8):
        loss = loss + lossb[k]
    loss_v[...] = loss * (1.0 / (8 * TOK))
    loss_copy = pltpu.make_async_copy(loss_v, out_loss, out_sem.at[0])
    loss_copy.start()


    acc = zr[0].astype(F32)
    came(zr.at[pl.ds(1, NZ - 1)], z_r)
    for r in range(1, NZ):
        acc = acc + zr[r].astype(F32)
    hidden_v[...] = jnp.concatenate([acc[0:24, :64], acc[0:24, 64:]], axis=0).astype(BF16)
    hidden_out = pltpu.make_async_copy(hidden_v, out_hidden, out_sem.at[1])
    hidden_out.start()

    gone(hv.at[0, 1], hs_sem.at[0])
    gone(hv.at[pl.ds(0, 2)], hs_sem.at[1])
    gone(psib, ss_sem)
    gone(enc_opp, rs_s.at[0])
    gone(enc_nb, rs_s.at[1])
    gone(psx.at[pl.ds(0, NX - 1)], px_s)
    gone(psz.at[pl.ds(0, NZ - 1)], pz_s)
    gone(lossb.at[pl.ds(0, 7)], ls_s)
    gone(gv.at[0, 0], ag_s.at[1])
    gone(gv.at[0, 0], ag_s.at[2])
    gone(gv.at[0, 0], ag_s.at[3])
    gone(gv.at[0], ag_s.at[4])
    gone(gv.at[0, 0], ag_s.at[5])
    gone(xr, x_s)
    gone(ys.at[pl.ds(1, 7)], y_s)
    gone(zr.at[pl.ds(1, NZ - 1)], z_s)
    pltpu.make_async_copy(head, out_head, head_sem).wait()
    loss_copy.wait()
    hidden_out.wait()


def per_device(hidden, head_weight, teacher_ids, teacher_logits):
    vm = pltpu.VMEM
    dma = pltpu.SemaphoreType.DMA
    scratch = [
        vm((TOK, K), jnp.int32),
        vm((TOK, K), F32),
        vm((VOCAB, FEAT), BF16),
        vm((NY, NC, TOK, FEAT), BF16),
        vm((NQ, NY, TOK, QC), F32),
        vm((NQ, NY, TOK, QC), F32),
        vm((NQ, NY, TOK, QC), F32),
        vm((NQ, TOK, QC), jnp.int16),
        vm((NQ, 2, TOK, QC), jnp.int16),
        vm((NQ, TOK, QC), jnp.int16),
        vm((NQ, 2, TOK, QC), jnp.int16),
        vm((TOK, K), F32),
        vm((TOK, NHI, 128), F32),
        vm((NHI, TOK, 128), F32),
        vm((NHI, TOK, 128), F32),
        vm((NX, 1, 128), F32),
        vm((NZ, 1, 128), F32),
        vm((8, 1, 128), F32),
        vm((NY, NC, TOK, VOCAB), BF16),
        vm((NY, NX, 2 * TOK, 128), F32),
        vm((NY, NX, 2 * TOK, 128), BF16),
        vm((NY, NX - 1, 2 * TOK, 128), BF16),
        vm((NY * NC, 64, 128), BF16),
        vm((NY, NC, 64, 128), BF16),
        vm((NZ, 32, 128), BF16),
        vm((VOCAB, FEAT), BF16),
        vm((TOK, D // 64), BF16),
        vm((1, 128), F32),
        dma((2,)), dma, dma, dma((3,)), dma((3,)), dma, dma((1 + 2 * NQ,)), dma((2,)), dma((NQ,)), dma((NQ,)),
        dma, dma, dma, dma, dma, dma, dma((6,)), dma((8,)), dma, dma((NY,)), dma, dma((NY,)), dma, dma, dma, dma((2,)),
        pltpu.SemaphoreType.REGULAR, pltpu.SemaphoreType.REGULAR,
    ]
    hbm = pl.BlockSpec(memory_space=pltpu.HBM)
    anys = pl.BlockSpec(memory_space=pl.ANY)
    hidden_grad, head_grad, loss = pl.pallas_call(
        kernel,
        out_shape=(
            pltpu.VMEM((TOK, D // 64), BF16),
            pltpu.VMEM((VOCAB, FEAT), BF16),
            pltpu.VMEM((1, 128), F32),
        ),
        in_specs=[hbm, hbm, hbm, hbm],
        out_specs=(anys, anys, anys),
        scratch_shapes=scratch,
        compiler_params=pltpu.CompilerParams(
            collective_id=0, has_side_effects=True, vmem_limit_bytes=56 * 1024 * 1024
        ),
    )(hidden, head_weight, teacher_ids, teacher_logits)
    return hidden_grad, head_grad, loss[0, 0]


def solution(mesh):
    in_specs = (P("dp", None), P("vocab", "dp"), P("dp", None), P("dp", None))
    out_specs = (P("dp", "vocab"), P("vocab", "dp"), P())
    return jax.shard_map(
        per_device, mesh=mesh, in_specs=in_specs, out_specs=out_specs, check_vma=False
    )
```

time: 75.6 us -> 70.1 us (0.927)
  the two profiles are of different devices: /device:TPU:48 before, /device:TPU:16 now
where the time goes in v3:
time: 70.1 us; the launch traced here: 69.7 us
  Pallas kernels  66 us (94%)
  local copies, waits for them, and re-layouts  1.92 us (3%)
  between operations  1.8 us (3%)
    pallas_call x1, Pallas kernels, per_device(): pl.pallas_call(kernel, out_shape=(pltpu.VMEM((TOK, D // 64), BF16), pltpu...  66 us
    unnamed x2, local copies, waits for them, and re-layouts  1.92 us

profile of v3, /device:TPU:16, one launch (start us, length us, event | category | flops | bytes accessed | tf_op | source)
XLA Modules:
  0.0 69.7 jit_solution(6919457937787900577)
XLA Ops:
  0.6 66.0 %shard_map.67 = (bf16[48,64]{1,0:T(8,128)(2,1)S(1)}, bf16[2048,512]{1,0:T(8,128)(2,1)S(1)}, f32[1,128]{1,0:T(1,128)S(1)}) custom-call(bf16[48,4096]{1,0:T(8,128)(2,1)} %hidden.1, bf16[2048,512]{1,0:T(8,128)(2,1)} %weight.1, s32[48,256]{1,0:T(8,128)} %ids_in.1, f32[48,256]{1,0:T(8,128)} %logits_in.1), custom_call_target="tpu_custom_call" | custom-call | tf_op jit(solution)/shard_map/pallas_call | solution.py:470
  66.7 0.6 copy.10
  67.3 1.3 %copy.11 = bf16[2048,512]{1,0:T(8,128)(2,1)} copy(bf16[2048,512]{1,0:T(8,128)(2,1)S(1)} %get-tuple-element.10) | data formatting | bytes 4194304

commit v4 on v3

--- a/solution.py
+++ b/solution.py
@@ -37,9 +37,9 @@
 def kernel(
     hidden, weight, ids_in, logits_in, out_hidden, out_head, out_loss,
     ids, logits, wv, hv, psib, pown, srecv, enc_opp, enc_nb, in_opp, in_nb,
-    prob, tgt, es, om, psx, psz, lossb, gv, gt, xs, xr, ys, yr, zr, head, hidden_v, loss_v,
+    prob, tgt, es, om, psz, lossb, gv, xs, xr, zs, zr, head, hidden_v, loss_v,
     id_sem, w_sem, own_sem, hs_sem, hr_sem, ss_sem, sr_sem, rs_s, rs_opp, rs_nb,
-    px_s, px_r, pz_s, pz_r, ls_s, ls_r, ag_s, ag_r, x_s, x_r, y_s, y_r, z_s, z_r, head_sem, out_sem, near2, near4,
+    pz_s, pz_r, ls_s, ls_r, ag_s, ag_r, x_s, x_r, z_s, z_r, head_sem, out_sem, near2, near4, near8,
 ):
     me = lax.axis_index("dp")
     vo = lax.axis_index("vocab")
@@ -66,6 +66,20 @@
 
     def gone(ref, sem):
         rc(ref, ref, sem, hr_sem.at[0], dp_dev(0, 1)).wait_send()
+
+    barrier = pltpu.get_barrier_semaphore()
+
+    def greet(dev):
+        pl.semaphore_signal(barrier, inc=1, device_id=dev, device_id_type=MESH)
+
+    for o in range(NY):
+        for cx in range(NC):
+            if o or cx:
+                greet(dp_dev(o, cx))
+    for r in range(1, NX):
+        greet(x_dev(r))
+    for r in (1, 2, NZ - 2, NZ - 1):
+        greet(z_dev((z + r) % NZ))
 
     w_copy = pltpu.make_async_copy(weight, wv, w_sem)
     own_h = pltpu.make_async_copy(hidden.at[:, pl.ds(pl.multiple_of(me * FEAT, FEAT), FEAT)], hv.at[0, 0], own_sem)
@@ -77,25 +91,12 @@
         w.start()
     w_copy.start()
 
-    barrier = pltpu.get_barrier_semaphore()
-
-    def greet(dev):
-        pl.semaphore_signal(barrier, inc=1, device_id=dev, device_id_type=MESH)
-
-    for o in range(NY):
-        for cx in range(NC):
-            if o or cx:
-                greet(dp_dev(o, cx))
-    for r in range(1, NX):
-        greet(x_dev(r))
-    for r in (1, 2, NZ - 2, NZ - 1):
-        greet(z_dev((z + r) % NZ))
-
     pl.semaphore_wait(barrier, 7 + (NX - 1) + 4)
 
-    def tell(sem, step):
-        for r in (step, NZ - step):
-            pl.semaphore_signal(sem, inc=1, device_id=z_dev((z + r) % NZ), device_id_type=MESH)
+    def tell(sem, *steps):
+        for step in steps:
+            for r in (step, NZ - step):
+                pl.semaphore_signal(sem, inc=1, device_id=z_dev((z + r) % NZ), device_id_type=MESH)
 
 
     def hidden_copy(o, cx):
@@ -107,7 +108,9 @@
 
     for o, cx in ((2, 0), (2, 1), (0, 1)):
         hidden_copy(o, cx).start()
-    tell(near2, 2)
+    tell(near2, 1, 2)
+    for r in range(1, NX):
+        pl.semaphore_signal(near2, inc=1, device_id=x_dev(r), device_id_type=MESH)
 
     for w in id_copies:
         w.wait()
@@ -135,6 +138,10 @@
             both = mm(jnp.concatenate([a1, a2, a3], axis=0), b, 1, 1)
             tgt[t] = both[0:NHI] + both[NHI:2 * NHI] + both[2 * NHI:3 * NHI]
 
+    pl.loop(0, 8)(target_tokens)
+    gone(hv.at[0], hs_sem.at[2])
+    for o, cx in ((1, 0), (3, 0), (1, 1), (3, 1)):
+        hidden_copy(o, cx).start()
 
     place_of = (0, 2, 1, 3)
 
@@ -172,55 +179,48 @@
         partial_logits(q, (0,))
         sib_copy(q, (0,)).start()
 
-    gone(hv.at[0], hs_sem.at[2])
-    for o, cx in ((1, 0), (3, 0), (1, 1), (3, 1)):
-        hidden_copy(o, cx).start()
-    pl.loop(0, TOK // 4)(target_tokens)
-    pl.semaphore_wait(near2, 2)
+    pl.loop(8, TOK // 4)(target_tokens)
+    pl.semaphore_wait(near2, 4 + NX - 1)
     tell(near4, 4)
     came(hv.at[2], hr_sem.at[2])
 
-    @pl.loop(0, NQ + 1)
+    @pl.loop(0, NQ)
+    def _(s):
+        q = q_of(s)
+        partial_logits(q, (2,))
+        sib_copy(q, (2,)).start()
+
+    came(hv.at[pl.ds(0, 2)], hr_sem.at[1])
+
+    @pl.loop(0, NQ + 4)
     def _(s):
         @pl.when(s < NQ)
         def _():
             q = q_of(s)
-            partial_logits(q, (2,))
-            sib_copy(q, (2,)).start()
-
-        @pl.when(s > 0)
-        def _():
-            q = q_of(s - 1)
             sib_copy(q, (2,)).wait_recv()
             enc_opp[q] = encode(pown[q, 1] + srecv[q, 1])
             opp_copy(q).start()
-
-    came(hv.at[pl.ds(0, 2)], hr_sem.at[1])
-
-    @pl.loop(0, NQ + 2)
-    def _(s):
-        @pl.when(s < NQ)
-        def _():
-            q = q_of(s)
             partial_logits(q, (1, 3))
             sib_copy(q, (1, 3)).start()
 
-        @pl.when(jnp.logical_and(s > 0, s <= NQ))
+        @pl.when(jnp.logical_and(s > 1, s <= NQ + 1))
         def _():
-            q = q_of(s - 1)
+            q = q_of(s - 2)
             sib_copy(q, (1, 3)).wait_recv()
             o = 4 - way(q)
             enc_nb[q, o // 2] = encode(pown[q, 2 + o // 2] + srecv[q, 2 + o // 2])
             nb_copy(q, o).start()
 
-        @pl.when(s > 1)
+        @pl.when(s > 3)
         def _():
-            q = q_of(s - 2)
+            q = q_of(s - 4)
             opp_copy(q).wait_recv()
             o = way(q)
             enc_nb[q, o // 2] = encode(pown[q, 2 + o // 2] + srecv[q, 2 + o // 2] + decode(in_opp[q]))
             nb_copy(q, o).start()
 
+    pl.semaphore_wait(near4, 2)
+    tell(near8, 4)
     tot = jnp.zeros((TOK, 128), F32)
     crs = jnp.zeros((TOK, 128), F32)
     came(srecv.at[:, 0], sr_sem.at[0])
@@ -247,18 +247,16 @@
     mine = jnp.where(lane == row, jnp.sum(tot, axis=1, keepdims=True), 0.0) + jnp.where(
         lane == row + 64, jnp.sum(crs, axis=1, keepdims=True), 0.0
     )
-    psx[x] = jnp.sum(mine, axis=0, keepdims=True)
-    for r in range(1, NX):
-        rc(psx.at[x], psx.at[x], px_s, px_r, x_dev(r)).start()
-    came(psx.at[pl.ds(0, NX - 1)], px_r)
-    pl.semaphore_wait(near4, 2)
-    psz[z] = psx[0] + psx[1] + psx[2] + psx[3]
-    for r in (8, 7, 9, 6, 10, 5, 11, 4, 12, 3, 13, 2, 14, 1, 15):
-        rc(psz.at[z], psz.at[z], pz_s, pz_r, z_dev((z + r) % NZ)).start()
-    came(psz.at[pl.ds(0, NZ - 1)], pz_r)
-    sums = psz[0]
-    for k in range(1, NZ):
-        sums = sums + psz[k]
+    psz[vo] = jnp.sum(mine, axis=0, keepdims=True)
+    pl.semaphore_wait(near8, 2)
+
+    @pl.loop(0, NZ * NX - 1)
+    def _(n):
+        there = (vo + 1 + (n + NZ * NX // 2 - 1) % (NZ * NX - 1)) % (NZ * NX)
+        rc(psz.at[vo], psz.at[vo], pz_s, pz_r, {"dp": me, "vocab": there}).start()
+
+    came(psz.at[pl.ds(0, NZ * NX - 1)], pz_r)
+    sums = jnp.sum(psz[...], axis=0)
     sums = jnp.broadcast_to(sums, (TOK, 128))
     total = jnp.sum(jnp.where(lane == row, sums, 0.0), axis=1, keepdims=True)
     cross = jnp.sum(jnp.where(lane == row + 64, sums, 0.0), axis=1, keepdims=True)
@@ -286,6 +284,18 @@
             if o or cx:
                 dev = dp_dev(o, cx)
                 rc(lossb.at[me], lossb.at[me], ls_s, ls_r, dev).start()
+
+    def send_terms(o):
+        for cx in range(NC):
+            for r in range(NX):
+                there = (x + r) % NX
+                src = xs.at[o, there, pl.ds(cx * TOK, TOK)]
+                slot = ((-o) % NY * NC + cx) * NX + (-r) % NX
+                if o or cx or r:
+                    dev = {"dp": dp_dev(o, cx)["dp"], "vocab": z * NX + there}
+                    rc(src, xr.at[slot], x_s, x_r.at[(-o) % NY], dev).start()
+                else:
+                    xr[0] = xs[0, x, 0:TOK]
 
     def terms(offsets):
         ga = jnp.concatenate([gv[o].reshape(NC * TOK, VOCAB) for o in offsets], axis=0)
@@ -295,78 +305,72 @@
             for m in range(NX):
                 cols = slice(m * 64, (m + 1) * 64)
                 piece = jnp.concatenate([part[0][rows, cols], part[1][rows, cols]], axis=1)
-                gt[o, m] = piece
                 xs[o, m] = piece.astype(BF16)
+            send_terms(o)
+
+    def to_z(o):
+        low = o * NC * NX
+        came(xr.at[pl.ds(low, 8)] if o else xr.at[pl.ds(1, 7)], x_r.at[o])
+        for cx in range(NC):
+            val = xr[low + cx * NX].astype(F32)
             for r in range(1, NX):
-                there = (x + r) % NX
-                rc(xs.at[o, there], xr.at[o, (-r) % NX - 1], x_s, x_r.at[o], x_dev(r)).start()
-
-    def to_y(o):
-        came(xr.at[o], x_r.at[o])
-        val = gt[o, x]
-        for r in range(NX - 1):
-            val = val + xr[o, r].astype(F32)
-        for cx in range(NC):
-            top, low = val[cx * TOK:cx * TOK + 24], val[cx * TOK + 24:(cx + 1) * TOK]
+                val = val + xr[low + cx * NX + r].astype(F32)
             gap = jnp.zeros((8, 128), F32)
-            mine = jnp.concatenate(
-                [
-                    jnp.concatenate([top[:, :64], low[:, :64]], axis=1), gap,
-                    jnp.concatenate([top[:, 64:], low[:, 64:]], axis=1), gap,
-                ],
-                axis=0,
-            ).astype(BF16)
-            if o or cx:
-                n = o * NC + cx
-                ys[n] = mine
-                back = (-o) % NY
-                rc(ys.at[n], yr.at[back, cx], y_s, y_r.at[back], dp_dev(o, cx)).start()
-            else:
-                yr[0, 0] = mine
-
-    def to_z(o):
-        came(yr.at[o] if o else yr.at[0, 1], y_r.at[o])
-        for cx in range(NC):
             for h in range(2):
+                cols = slice(h * 64, (h + 1) * 64)
+                part = jnp.concatenate([val[0:24, cols], val[24:48, cols]], axis=1)
+                zs[o, cx, h] = jnp.concatenate([part, gap], axis=0).astype(BF16)
                 zd = 2 * dp_dev(o, cx)["dp"] + h
                 r = (z - zd + NZ) % NZ
-                part = yr.at[o, cx, pl.ds(32 * h, 32)]
-                copy = rc(part, zr.at[r], z_s, z_r, z_dev(zd))
                 here = r == 0
 
                 @pl.when(jnp.logical_not(here))
                 def _():
-                    copy.start()
+                    rc(zs.at[o, cx, h], zr.at[r], z_s, z_r, z_dev(zd)).start()
 
                 @pl.when(here)
                 def _():
-                    zr[0] = yr[o, cx, 32 * h:32 * h + 32]
-
-    gone(gv.at[0, 0], ag_s.at[0])
-    pass_on(0, 1, 1, 0, 2, 3)
-    pass_on(0, 0, 3, 0, 2, 3)
+                    zr[0] = zs[o, cx, h]
+
+    def second_halves():
+        pass_on(0, 1, 1, 0, 2, 3)
+        pass_on(0, 0, 3, 0, 2, 3)
+
+    def far_halves():
+        for h in range(2):
+            came(gv.at[2, 0, :, half[h]], ag_r.at[4 + h])
+            pass_on(2, h, 0, 1, 5, 7)
+
+
+    @pl.when(c == 0)
+    def _():
+        gone(gv.at[0, 0], ag_s.at[0])
+        second_halves()
+
     came(gv.at[3, 0, :, half[0]], ag_r.at[0])
     pass_on(3, 0, 1, 0, 3, 4)
     pass_on(3, 0, 0, 1, 4, 6)
     came(gv.at[1, 0, :, half[1]], ag_r.at[1])
     pass_on(1, 1, 3, 0, 3, 5)
     pass_on(1, 1, 0, 1, 4, 6)
+
+    @pl.when(c == 1)
+    def _():
+        gone(gv.at[0, 0], ag_s.at[0])
+        second_halves()
+
     came(gv.at[0, 1], ag_r.at[2])
     terms((0,))
     came(gv.at[0, 0], ag_r.at[3])
     pass_on(3, 1, 0, 1, 4, 6)
     pass_on(1, 0, 0, 1, 4, 6)
+    pl.when(c == 1)(far_halves)
     came(gv.at[0], ag_r.at[6])
     terms((1, 3))
-    for h in range(2):
-        came(gv.at[2, 0, :, half[h]], ag_r.at[4 + h])
-        pass_on(2, h, 0, 1, 5, 7)
-    to_y(0)
+    pl.when(c == 0)(far_halves)
+    to_z(0)
     came(gv.at[2, 1], ag_r.at[7])
     terms((2,))
-    to_z(0)
-    to_y(1)
-    to_y(3)
 
     HB = 256
 
@@ -384,13 +388,12 @@
             head_copy(n).start()
 
     nh = VOCAB // HB
-    head_part(0, 2)
-    to_y(2)
+    head_part(0, 3)
     to_z(3)
     to_z(1)
-    head_part(2, 4)
+    head_part(3, 5)
     to_z(2)
-    head_part(4, nh)
+    head_part(5, nh)
     came(lossb.at[pl.ds(0, 7)], ls_r)
     loss = lossb[0]
     for k in range(1, 8):
@@ -413,16 +416,14 @@
     gone(psib, ss_sem)
     gone(enc_opp, rs_s.at[0])
     gone(enc_nb, rs_s.at[1])
-    gone(psx.at[pl.ds(0, NX - 1)], px_s)
-    gone(psz.at[pl.ds(0, NZ - 1)], pz_s)
+    gone(psz.at[pl.ds(0, NZ * NX - 1)], pz_s)
     gone(lossb.at[pl.ds(0, 7)], ls_s)
     gone(gv.at[0, 0], ag_s.at[1])
     gone(gv.at[0, 0], ag_s.at[2])
     gone(gv.at[0, 0], ag_s.at[3])
     gone(gv.at[0], ag_s.at[4])
     gone(gv.at[0, 0], ag_s.at[5])
-    gone(xr, x_s)
-    gone(ys.at[pl.ds(1, 7)], y_s)
+    gone(xr.at[pl.ds(1, 31)], x_s)
     gone(zr.at[pl.ds(1, NZ - 1)], z_s)
     pltpu.make_async_copy(head, out_head, head_sem).wait()
     loss_copy.wait()
@@ -448,22 +449,19 @@
         vm((TOK, NHI, 128), F32),
         vm((NHI, TOK, 128), F32),
         vm((NHI, TOK, 128), F32),
-        vm((NX, 1, 128), F32),
-        vm((NZ, 1, 128), F32),
+        vm((NZ * NX, 1, 128), F32),
         vm((8, 1, 128), F32),
         vm((NY, NC, TOK, VOCAB), BF16),
-        vm((NY, NX, 2 * TOK, 128), F32),
         vm((NY, NX, 2 * TOK, 128), BF16),
-        vm((NY, NX - 1, 2 * TOK, 128), BF16),
-        vm((NY * NC, 64, 128), BF16),
-        vm((NY, NC, 64, 128), BF16),
+        vm((NY * NC * NX, TOK, 128), BF16),
+        vm((NY, NC, 2, 32, 128), BF16),
         vm((NZ, 32, 128), BF16),
         vm((VOCAB, FEAT), BF16),
         vm((TOK, D // 64), BF16),
         vm((1, 128), F32),
         dma((2,)), dma, dma, dma((3,)), dma((3,)), dma, dma((1 + 2 * NQ,)), dma((2,)), dma((NQ,)), dma((NQ,)),
-        dma, dma, dma, dma, dma, dma, dma((6,)), dma((8,)), dma, dma((NY,)), dma, dma((NY,)), dma, dma, dma, dma((2,)),
-        pltpu.SemaphoreType.REGULAR, pltpu.SemaphoreType.REGULAR,
+        dma, dma, dma, dma, dma((6,)), dma((8,)), dma, dma((NY,)), dma, dma, dma, dma((2,)),
+        pltpu.SemaphoreType.REGULAR, pltpu.SemaphoreType.REGULAR, pltpu.SemaphoreType.REGULAR,
     ]
     hbm = pl.BlockSpec(memory_space=pltpu.HBM)
     anys = pl.BlockSpec(memory_space=pl.ANY)

time: 70.1 us -> 67.2 us (0.959)
  Pallas kernels: 66 us -> 63.1 us
    pallas_call x1, Pallas kernels: 66 us -> 63.1 us  [per_device(): pl.pallas_call(kernel, out_shape=(pltpu.VMEM((TOK, D // 64), BF16), pltpu...]
where the time goes in v4:
time: 67.2 us; the launch traced here: 66.8 us
  Pallas kernels  63.1 us (94%)
  local copies, waits for them, and re-layouts  1.92 us (3%)
  between operations  1.8 us (3%)
    pallas_call x1, Pallas kernels, per_device(): pl.pallas_call(kernel, out_shape=(pltpu.VMEM((TOK, D // 64), BF16), pltpu...  63.1 us
    unnamed x2, local copies, waits for them, and re-layouts  1.92 us

profile of v4, /device:TPU:16, one launch (start us, length us, event | category | flops | bytes accessed | tf_op | source)
XLA Modules:
  0.0 66.8 jit_solution(8517583739451436023)
XLA Ops:
  0.6 63.1 %shard_map.67 = (bf16[48,64]{1,0:T(8,128)(2,1)S(1)}, bf16[2048,512]{1,0:T(8,128)(2,1)S(1)}, f32[1,128]{1,0:T(1,128)S(1)}) custom-call(bf16[48,4096]{1,0:T(8,128)(2,1)} %hidden.1, bf16[2048,512]{1,0:T(8,128)(2,1)} %weight.1, s32[48,256]{1,0:T(8,128)} %ids_in.1, f32[48,256]{1,0:T(8,128)} %logits_in.1), custom_call_target="tpu_custom_call" | custom-call | tf_op jit(solution)/shard_map/pallas_call | solution.py:468
  63.7 0.6 copy.10
  64.3 1.3 %copy.11 = bf16[2048,512]{1,0:T(8,128)(2,1)} copy(bf16[2048,512]{1,0:T(8,128)(2,1)S(1)} %get-tuple-element.10) | data formatting | bytes 4194304

commit v5 on v4

--- a/solution.py
+++ b/solution.py
@@ -139,7 +139,6 @@
             tgt[t] = both[0:NHI] + both[NHI:2 * NHI] + both[2 * NHI:3 * NHI]
 
     pl.loop(0, 8)(target_tokens)
-    gone(hv.at[0], hs_sem.at[2])
     for o, cx in ((1, 0), (3, 0), (1, 1), (3, 1)):
         hidden_copy(o, cx).start()
 
@@ -190,16 +189,21 @@
         partial_logits(q, (2,))
         sib_copy(q, (2,)).start()
 
+
+    @pl.loop(0, NQ)
+    def _(s):
+        q = q_of(s)
+        sib_copy(q, (2,)).wait_recv()
+        enc_opp[q] = encode(pown[q, 1] + srecv[q, 1])
+        opp_copy(q).start()
+
     came(hv.at[pl.ds(0, 2)], hr_sem.at[1])
 
-    @pl.loop(0, NQ + 4)
+    @pl.loop(0, NQ + 3)
     def _(s):
         @pl.when(s < NQ)
         def _():
             q = q_of(s)
-            sib_copy(q, (2,)).wait_recv()
-            enc_opp[q] = encode(pown[q, 1] + srecv[q, 1])
-            opp_copy(q).start()
             partial_logits(q, (1, 3))
             sib_copy(q, (1, 3)).start()
 
@@ -211,9 +215,9 @@
             enc_nb[q, o // 2] = encode(pown[q, 2 + o // 2] + srecv[q, 2 + o // 2])
             nb_copy(q, o).start()
 
-        @pl.when(s > 3)
+        @pl.when(s > 2)
         def _():
-            q = q_of(s - 4)
+            q = q_of(s - 3)
             opp_copy(q).wait_recv()
             o = way(q)
             enc_nb[q, o // 2] = encode(pown[q, 2 + o // 2] + srecv[q, 2 + o // 2] + decode(in_opp[q]))
@@ -252,7 +256,7 @@
 
     @pl.loop(0, NZ * NX - 1)
     def _(n):
-        there = (vo + 1 + (n + NZ * NX // 2 - 1) % (NZ * NX - 1)) % (NZ * NX)
+        there = (vo + NZ * NX // 2 + (1 - 2 * (n % 2)) * ((n + 1) // 2)) % (NZ * NX)
         rc(psz.at[vo], psz.at[vo], pz_s, pz_r, {"dp": me, "vocab": there}).start()
 
     came(psz.at[pl.ds(0, NZ * NX - 1)], pz_r)
@@ -342,9 +346,15 @@
             pass_on(2, h, 0, 1, 5, 7)
 
 
+    def terms_own():
+        came(gv.at[0, 1], ag_r.at[2])
+        terms((0,))
+
+    pl.when(c == 1)(second_halves)
+
     @pl.when(c == 0)
     def _():
-        gone(gv.at[0, 0], ag_s.at[0])
+        terms_own()
         second_halves()
 
     came(gv.at[3, 0, :, half[0]], ag_r.at[0])
@@ -353,14 +363,7 @@
     came(gv.at[1, 0, :, half[1]], ag_r.at[1])
     pass_on(1, 1, 3, 0, 3, 5)
     pass_on(1, 1, 0, 1, 4, 6)
-
-    @pl.when(c == 1)
-    def _():
-        gone(gv.at[0, 0], ag_s.at[0])
-        second_halves()
-
-    came(gv.at[0, 1], ag_r.at[2])
-    terms((0,))
+    pl.when(c == 1)(terms_own)
     came(gv.at[0, 0], ag_r.at[3])
     pass_on(3, 1, 0, 1, 4, 6)
     pass_on(1, 0, 0, 1, 4, 6)
@@ -412,12 +415,14 @@
     hidden_out.start()
 
     gone(hv.at[0, 1], hs_sem.at[0])
+    gone(hv.at[0], hs_sem.at[2])
     gone(hv.at[pl.ds(0, 2)], hs_sem.at[1])
     gone(psib, ss_sem)
     gone(enc_opp, rs_s.at[0])
     gone(enc_nb, rs_s.at[1])
     gone(psz.at[pl.ds(0, NZ * NX - 1)], pz_s)
     gone(lossb.at[pl.ds(0, 7)], ls_s)
+    gone(gv.at[0, 0], ag_s.at[0])
     gone(gv.at[0, 0], ag_s.at[1])
     gone(gv.at[0, 0], ag_s.at[2])
     gone(gv.at[0, 0], ag_s.at[3])

time: 67.2 us -> 62.9 us (0.936)
  Pallas kernels: 63.1 us -> 59 us
    pallas_call x1, Pallas kernels: 63.1 us -> 59 us  [per_device(): pl.pallas_call(kernel, out_shape=(pltpu.VMEM((TOK, D // 64), BF16), pltpu...]
where the time goes in v5:
time: 62.9 us; the launch traced here: 62.7 us
  Pallas kernels  59 us (94%)
  local copies, waits for them, and re-layouts  1.92 us (3%)
  between operations  1.8 us (3%)
    pallas_call x1, Pallas kernels, per_device(): pl.pallas_call(kernel, out_shape=(pltpu.VMEM((TOK, D // 64), BF16), pltpu...  59 us
    unnamed x2, local copies, waits for them, and re-layouts  1.92 us

profile of v5, /device:TPU:16, one launch (start us, length us, event | category | flops | bytes accessed | tf_op | source)
XLA Modules:
  0.0 62.7 jit_solution(13036185299972198001)
XLA Ops:
  0.6 59.0 %shard_map.67 = (bf16[48,64]{1,0:T(8,128)(2,1)S(1)}, bf16[2048,512]{1,0:T(8,128)(2,1)S(1)}, f32[1,128]{1,0:T(1,128)S(1)}) custom-call(bf16[48,4096]{1,0:T(8,128)(2,1)} %hidden.1, bf16[2048,512]{1,0:T(8,128)(2,1)} %weight.1, s32[48,256]{1,0:T(8,128)} %ids_in.1, f32[48,256]{1,0:T(8,128)} %logits_in.1), custom_call_target="tpu_custom_call" | custom-call | tf_op jit(solution)/shard_map/pallas_call | solution.py:473
  59.7 0.6 copy.10
  60.3 1.3 %copy.11 = bf16[2048,512]{1,0:T(8,128)(2,1)} copy(bf16[2048,512]{1,0:T(8,128)(2,1)S(1)} %get-tuple-element.10) | data formatting | bytes 4194304

commit v6 on v5

--- a/solution.py
+++ b/solution.py
@@ -35,11 +35,11 @@
 
 
 def kernel(
-    hidden, weight, ids_in, logits_in, out_hidden, out_head, out_loss,
+    hidden, weight, ids_in, logits_in, out_small, out_head,
     ids, logits, wv, hv, psib, pown, srecv, enc_opp, enc_nb, in_opp, in_nb,
-    prob, tgt, es, om, psz, lossb, gv, xs, xr, zs, zr, head, hidden_v, loss_v,
+    prob, tgt, es, om, psz, lossb, gv, xs, xr, zs, zr, head,
     id_sem, w_sem, own_sem, hs_sem, hr_sem, ss_sem, sr_sem, rs_s, rs_opp, rs_nb,
-    pz_s, pz_r, ls_s, ls_r, ag_s, ag_r, x_s, x_r, z_s, z_r, head_sem, out_sem, near2, near4, near8,
+    pz_s, pz_r, ls_s, ls_r, ag_s, ag_r, x_s, x_r, z_s, z_r, head_sem, near2, near4, near8,
 ):
     me = lax.axis_index("dp")
     vo = lax.axis_index("vocab")
@@ -401,18 +401,14 @@
     loss = lossb[0]
     for k in range(1, 8):
         loss = loss + lossb[k]
-    loss_v[...] = loss * (1.0 / (8 * TOK))
-    loss_copy = pltpu.make_async_copy(loss_v, out_loss, out_sem.at[0])
-    loss_copy.start()
 
 
     acc = zr[0].astype(F32)
     came(zr.at[pl.ds(1, NZ - 1)], z_r)
     for r in range(1, NZ):
         acc = acc + zr[r].astype(F32)
-    hidden_v[...] = jnp.concatenate([acc[0:24, :64], acc[0:24, 64:]], axis=0).astype(BF16)
-    hidden_out = pltpu.make_async_copy(hidden_v, out_hidden, out_sem.at[1])
-    hidden_out.start()
+    out_small[0:24, :] = acc[0:24]
+    out_small[24:32, :] = jnp.broadcast_to(loss * (1.0 / (8 * TOK)), (8, 128))
 
     gone(hv.at[0, 1], hs_sem.at[0])
     gone(hv.at[0], hs_sem.at[2])
@@ -431,8 +427,6 @@
     gone(xr.at[pl.ds(1, 31)], x_s)
     gone(zr.at[pl.ds(1, NZ - 1)], z_s)
     pltpu.make_async_copy(head, out_head, head_sem).wait()
-    loss_copy.wait()
-    hidden_out.wait()
 
 
 def per_device(hidden, head_weight, teacher_ids, teacher_logits):
@@ -462,29 +456,28 @@
         vm((NY, NC, 2, 32, 128), BF16),
         vm((NZ, 32, 128), BF16),
         vm((VOCAB, FEAT), BF16),
-        vm((TOK, D // 64), BF16),
-        vm((1, 128), F32),
         dma((2,)), dma, dma, dma((3,)), dma((3,)), dma, dma((1 + 2 * NQ,)), dma((2,)), dma((NQ,)), dma((NQ,)),
-        dma, dma, dma, dma, dma((6,)), dma((8,)), dma, dma((NY,)), dma, dma, dma, dma((2,)),
+        dma, dma, dma, dma, dma((6,)), dma((8,)), dma, dma((NY,)), dma, dma, dma,
         pltpu.SemaphoreType.REGULAR, pltpu.SemaphoreType.REGULAR, pltpu.SemaphoreType.REGULAR,
     ]
     hbm = pl.BlockSpec(memory_space=pltpu.HBM)
     anys = pl.BlockSpec(memory_space=pl.ANY)
-    hidden_grad, head_grad, loss = pl.pallas_call(
+    vmem = pl.BlockSpec(memory_space=pltpu.VMEM)
+    small, head_grad = pl.pallas_call(
         kernel,
         out_shape=(
-            pltpu.VMEM((TOK, D // 64), BF16),
+            pltpu.VMEM((32, 128), F32),
             pltpu.VMEM((VOCAB, FEAT), BF16),
-            pltpu.VMEM((1, 128), F32),
         ),
         in_specs=[hbm, hbm, hbm, hbm],
-        out_specs=(anys, anys, anys),
+        out_specs=(vmem, anys),
         scratch_shapes=scratch,
         compiler_params=pltpu.CompilerParams(
             collective_id=0, has_side_effects=True, vmem_limit_bytes=56 * 1024 * 1024
         ),
     )(hidden, head_weight, teacher_ids, teacher_logits)
-    return hidden_grad, head_grad, loss[0, 0]
+    hidden_grad = jnp.concatenate([small[:24, :64], small[:24, 64:]], axis=0).astype(BF16)
+    return hidden_grad, head_grad, small[24, 0]
 
 
 def solution(mesh):

time: 62.9 us -> 62.2 us (0.989)
  between operations: 1.8 us -> 0.65 us
    unnamed x2 -> x1, local copies, waits for them, and re-layouts: 1.92 us -> 1.32 us
where the time goes in v6:
time: 62.2 us; the launch traced here: 62.1 us
  Pallas kernels  58.9 us (95%)
  local copies, waits for them, and re-layouts  1.9 us (3%)
  between operations  0.65 us (1%)
    pallas_call x1, Pallas kernels, per_device(): pl.pallas_call(kernel, out_shape=(pltpu.VMEM((32, 128), F32), pltpu.VMEM(...  58.9 us
    unnamed x1, local copies, waits for them, and re-layouts  1.32 us

profile of v6, /device:TPU:16, one launch (start us, length us, event | category | flops | bytes accessed | tf_op | source)
XLA Modules:
  0.0 62.1 jit_solution(3885045035540634659)
XLA Ops:
  0.6 58.9 %shard_map.67 = (f32[32,128]{1,0:T(8,128)S(1)}, bf16[2048,512]{1,0:T(8,128)(2,1)S(1)}) custom-call(bf16[48,4096]{1,0:T(8,128)(2,1)} %hidden.1, bf16[2048,512]{1,0:T(8,128)(2,1)} %weight.1, s32[48,256]{1,0:T(8,128)} %ids_in.1, f32[48,256]{1,0:T(8,128)} %logits_in.1), custom_call_target="tpu_custom_call" | custom-call | tf_op jit(solution)/shard_map/pallas_call | solution.py:466
  59.6 0.1 fusion
  59.6 0.6 pad_maximum_fusion
  60.3 0.5 slice.13
  60.8 1.3 %copy.8 = bf16[2048,512]{1,0:T(8,128)(2,1)} copy(bf16[2048,512]{1,0:T(8,128)(2,1)S(1)} %get-tuple-element.10) | data formatting | bytes 4194304
  (1 shorter events, 0.0 us)

commit v7 on v6

--- a/solution.py
+++ b/solution.py
@@ -270,6 +270,7 @@
         gv[0, 0, :, hi * 128:(hi + 1) * 128] = g.astype(BF16)
 
     half = [pl.ds(0, VOCAB // 2), pl.ds(VOCAB // 2, VOCAB // 2)]
+    half += [pl.ds(n * (VOCAB // 4), VOCAB // 4) for n in range(4)]
 
     def pass_on(o, h, do, dcx, ssem, rsem):
         back = (o - do) % NY
@@ -277,8 +278,10 @@
         dst = gv.at[back, dcx] if h is None else gv.at[back, dcx, :, half[h]]
         rc(src, dst, ag_s.at[ssem], ag_r.at[rsem], dp_dev(do, dcx)).start()
 
-    pass_on(0, 0, 1, 0, 0, 0)
-    pass_on(0, 1, 3, 0, 0, 1)
+    pass_on(0, 2, 1, 0, 0, 0)
+    pass_on(0, 4, 3, 0, 0, 1)
+    pass_on(0, 3, 1, 0, 0, 8)
+    pass_on(0, 5, 3, 0, 0, 9)
     pass_on(0, None, 0, 1, 1, 2)
 
     token_loss = entropy - cross + jnp.log(total)
@@ -357,11 +360,12 @@
         terms_own()
         second_halves()
 
-    came(gv.at[3, 0, :, half[0]], ag_r.at[0])
-    pass_on(3, 0, 1, 0, 3, 4)
+    for n in range(2):
+        came(gv.at[3, 0, :, half[2 + n]], ag_r.at[8 * n])
+        pass_on(3, 2 + n, 1, 0, 3, 4)
+        came(gv.at[1, 0, :, half[4 + n]], ag_r.at[1 + 8 * n])
+        pass_on(1, 4 + n, 3, 0, 3, 5)
     pass_on(3, 0, 0, 1, 4, 6)
-    came(gv.at[1, 0, :, half[1]], ag_r.at[1])
-    pass_on(1, 1, 3, 0, 3, 5)
     pass_on(1, 1, 0, 1, 4, 6)
     pl.when(c == 1)(terms_own)
     came(gv.at[0, 0], ag_r.at[3])
@@ -457,7 +461,7 @@
         vm((NZ, 32, 128), BF16),
         vm((VOCAB, FEAT), BF16),
         dma((2,)), dma, dma, dma((3,)), dma((3,)), dma, dma((1 + 2 * NQ,)), dma((2,)), dma((NQ,)), dma((NQ,)),
-        dma, dma, dma, dma, dma((6,)), dma((8,)), dma, dma((NY,)), dma, dma, dma,
+        dma, dma, dma, dma, dma((6,)), dma((10,)), dma, dma((NY,)), dma, dma, dma,
         pltpu.SemaphoreType.REGULAR, pltpu.SemaphoreType.REGULAR, pltpu.SemaphoreType.REGULAR,
     ]
     hbm = pl.BlockSpec(memory_space=pltpu.HBM)

time: 62.2 us -> 62.8 us (level)
  no operation moved by 1% of the time
where the time goes in v7:
time: 62.8 us; the launch traced here: 62.7 us
  Pallas kernels  59.5 us (95%)
  local copies, waits for them, and re-layouts  1.9 us (3%)
  between operations  0.65 us (1%)
    pallas_call x1, Pallas kernels, per_device(): pl.pallas_call(kernel, out_shape=(pltpu.VMEM((32, 128), F32), pltpu.VMEM(...  59.5 us
    unnamed x1, local copies, waits for them, and re-layouts  1.32 us

profile of v7, /device:TPU:16, one launch (start us, length us, event | category | flops | bytes accessed | tf_op | source)
XLA Modules:
  0.0 62.7 jit_solution(15912871775642801038)
XLA Ops:
  0.6 59.5 %shard_map.67 = (f32[32,128]{1,0:T(8,128)S(1)}, bf16[2048,512]{1,0:T(8,128)(2,1)S(1)}) custom-call(bf16[48,4096]{1,0:T(8,128)(2,1)} %hidden.1, bf16[2048,512]{1,0:T(8,128)(2,1)} %weight.1, s32[48,256]{1,0:T(8,128)} %ids_in.1, f32[48,256]{1,0:T(8,128)} %logits_in.1), custom_call_target="tpu_custom_call" | custom-call | tf_op jit(solution)/shard_map/pallas_call | solution.py:470
  60.2 0.1 fusion
  60.2 0.6 pad_maximum_fusion
  60.9 0.5 slice.13
  61.4 1.3 %copy.8 = bf16[2048,512]{1,0:T(8,128)(2,1)} copy(bf16[2048,512]{1,0:T(8,128)(2,1)S(1)} %get-tuple-element.10) | data formatting | bytes 4194304
  (1 shorter events, 0.0 us)
